TPU v7x, 512 devices: a whole 4x4x16 slice. The times are simulated.
512 devices in a mesh: dp: 32 (over y, x, z_hi), tensor: 16 (over z_lo, core).
Axes of the slice: x: 4, y: 4, z: 16 (z_hi: 2, z_lo: 8; z = z_hi * 8 + z_lo), core: 2. Of those that a mesh axis runs over, the one named last changes fastest.
Arguments:
- grads: bfloat16 [32, 6144, 512], P(None, ('tensor', 'dp')), may hold values from -100 to 100
- d_query: bfloat16 [4096, 6144], P('dp', 'tensor'), may hold values from -6 to 6
- w_query: bfloat16 [6144, 6144], P('dp', 'tensor'), may hold values from -0.078125 to 0.078125
Outputs:
- updates: float32 [32, 6144, 512], P(None, ('tensor', 'dp'))
- d_input: float32 [4096, 6144], P('dp', 'tensor')
All inputs are finite; a program needn't handle non-finite values.
Results may differ from a plain program's by a relative error of at most 0.0005.
Values may be sent and summed in bfloat16 or wider, within the bound.
No kernel may reach another device: no remote copies, remote signals or barrier semaphores. Data moves between devices by JAX's collectives and lax.ppermute only.
A program may use at most 64 MiB of HBM per device.

v0:
```python
import math

import jax
import jax.numpy as jnp
from jax import lax
from jax.sharding import PartitionSpec as P

D = 6144
ITERS = 3


COEF_A = 3.4445
COEF_B = -4.775
COEF_C = 2.0315
HIGH = lax.Precision.HIGHEST


def owner_work(received):
    local = received[0]
    wide = local.astype(jnp.float32)
    local_squares = jnp.sum(wide * wide, axis=(1, 2))
    total = lax.psum(local_squares, "tensor")
    ortho = wide / (jnp.sqrt(total)[:, None, None] + 1e-07)
    factor = math.sqrt(D)
    result = ortho
    for step in range(ITERS):
        part = jnp.einsum(
            "nrk,nrj->nkj", ortho, ortho, preferred_element_type=jnp.float32, precision=HIGH
        )
        gram = lax.psum(part, "tensor")
        squared = jnp.einsum(
            "nkj,nji->nki", gram, gram, preferred_element_type=jnp.float32, precision=HIGH
        )
        poly = COEF_B * gram + COEF_C * squared
        moved = jnp.einsum(
            "nrk,nkj->nrj", ortho, poly, preferred_element_type=jnp.float32, precision=HIGH
        )
        following = COEF_A * ortho + moved
        if step + 1 < ITERS:
            ortho = following
        else:
            result = factor * following
    return lax.all_to_all(result[None], "dp", split_axis=2, concat_axis=0, tiled=True)


def body(grads, d_query, w_query):
    dp_count = lax.axis_size("dp")
    local_count = grads.shape[0]
    owned_count = local_count // dp_count
    sectioned = grads.reshape(dp_count, owned_count, grads.shape[1], grads.shape[2])
    returned = owner_work(lax.all_to_all(sectioned, "dp", split_axis=0, concat_axis=2, tiled=True))
    updates = returned.reshape(local_count, grads.shape[1], grads.shape[2])
    token_count = d_query.shape[0]
    all_terms = lax.dot_general(
        lax.all_gather(d_query, "dp", axis=0, tiled=True),
        w_query,
        (((1,), (1,)), ((), ())),
        preferred_element_type=jnp.float32,
    )
    routed = lax.all_to_all(
        all_terms.reshape(dp_count, token_count, w_query.shape[0]),
        "dp",
        split_axis=0,
        concat_axis=2,
        tiled=True,
    )
    partial_sum = routed.reshape(token_count, dp_count * w_query.shape[0])
    d_input = lax.psum_scatter(partial_sum, "tensor", scatter_dimension=1, tiled=True)
    return (updates, d_input)


def solution(mesh):
    return jax.shard_map(
        body,
        mesh=mesh,
        in_specs=(P(None, ("tensor", "dp"), None), P("dp", "tensor"), P("dp", "tensor")),
        out_specs=(P(None, ("tensor", "dp"), None), P("dp", "tensor")),
        check_vma=False,
    )
```

profile of v0, /device:TPU:1, one launch (start us, length us, event | category | flops | bytes accessed | tf_op | source)
XLA Modules:
  0.0 1121.6 jit_solution(13327229002741934209)
XLA Ops:
  8.0 0.0 copy-start
  8.0 0.0 all-gather.2.cloned.1.call-start
  8.1 0.7 all-gather.2.cloned.1.call-update
  8.7 2.0 copy.32
  10.8 21.2 %all-to-all-start = ((bf16[32,1,12,512]{3,2,1,0:T(8,128)(2,1)}), bf16[32,1,12,512]{3,2,1,0:T(8,128)(2,1)}, u32[]{:S(2)}, u32[]{:S(2)}) async-start(bf16[32,1,12,512]{3,2,1,0:T(8,128)(2,1)} %bitcast.75), calls=%async_computation | async-start | bytes 1048576 | tf_op jit(solution)/shard_map/all_to_all | solution.py:51
  32.0 147.1 %all-gather.2.cloned.1.call-done = bf16[4096,384]{1,0:T(8,128)(2,1)} async-done(((bf16[128,384]{1,0:T(8,128)(2,1)}), bf16[4096,384]{1,0:T(8,128)(2,1)}) %all-gather.2.cloned.1.call-update) | async-done | bytes 3145744 | tf_op jit(solution)/shard_map/all_gather | solution.py:55
  179.1 0.0 copy-done
  179.1 3.1 convolution_bitcast_fusion
  182.3 2.0 copy.31
  184.3 0.0 all-to-all-done
  184.3 5.3 all-to-all-start.2
  189.6 0.0 all-reduce.4.cloned.1.call-start
  189.6 1.9 fusion.14
  191.5 168.1 %psum.28 = f32[1]{0:T(128)} all-reduce(f32[1]{0:T(128)} %bitcast.1), channel_id=1, replica_groups=mesh['dp'=32,'tensor'=16] {'tensor'}, use_global_device_ids=true, to_apply=%region_1.0 | all-reduce | flops 1 | bytes 8 | tf_op jit(solution)/shard_map/psum | solution.py:22
  360.3 4.5 convolution_bitcast_fusion.3
  364.8 0.0 all-reduce.4.cloned.1.call-update
  364.8 0.0 all-reduce.6.cloned.1.call-start
  364.9 2.2 convert_divide_fusion
  367.1 1.5 copy.15
  368.6 2.2 div.33
  370.7 2.6 copy.14
  373.3 2.2 mul.60
  375.5 196.1 %all-reduce.4.cloned.1.call-done = f32[1,512,512]{2,1,0:T(8,128)} async-done(((f32[1,512,512]{2,1,0:T(8,128)}), f32[1,512,512]{2,1,0:T(8,128)}) %all-reduce.4.cloned.1.call-update) | async-done | bytes 1048592 | tf_op jit(solution)/shard_map/psum | solution.py:30
  571.6 3.9 fusion.4
  575.5 2.8 convolution_add_fusion.2
  578.3 0.0 copy-start.3
  578.3 0.9 copy-done.3
  579.2 2.8 convolution_bitcast_fusion.2
  582.0 0.0 all-reduce.6.cloned.1.call-update
  582.0 0.2 all-reduce.8.cloned.1.call-start
  582.3 199.2 %all-reduce.6.cloned.1.call-done = f32[1,512,512]{2,1,0:T(8,128)} async-done(((f32[1,512,512]{2,1,0:T(8,128)}), f32[1,512,512]{2,1,0:T(8,128)}) %all-reduce.6.cloned.1.call-update) | async-done | bytes 1048592 | tf_op jit(solution)/shard_map/psum | solution.py:30
  781.5 3.9 fusion.6
  785.4 2.8 convolution_add_fusion.1
  788.2 0.0 copy-start.2
  788.2 0.9 copy-done.2
  789.1 2.8 convolution_bitcast_fusion.1
  791.9 0.0 all-reduce.8.cloned.1.call-update
  791.9 0.0 reduce-scatter.2.cloned.1.call-start
  792.0 0.0 all-to-all-done.2
  792.0 0.0 copy-start.1
  792.0 1.6 copy-done.1
  793.7 0.0 reduce-scatter.2.cloned.1.call-update
  793.7 197.8 %all-reduce.8.cloned.1.call-done = f32[1,512,512]{2,1,0:T(8,128)} async-done(((f32[1,512,512]{2,1,0:T(8,128)}), f32[1,512,512]{2,1,0:T(8,128)}) %all-reduce.8.cloned.1.call-update) | async-done | bytes 1048592 | tf_op jit(solution)/shard_map/psum | solution.py:30
  991.5 3.9 fusion.8
  995.4 2.8 fusion.10
  998.2 0.8 copy.16
  999.0 43.9 %all_to_all.33 = f32[1,1,384,512]{3,1,0,2:T(1,128)S(1)} all-to-all(f32[1,1,384,512]{3,1,0,2:T(1,128)S(1)} %copy.16), channel_id=1, replica_groups=mesh['dp'=32,'tensor'=16] {'dp'}, dimensions={2} | all-to-all | bytes 1572864 | tf_op jit(solution)/shard_map/all_to_all | solution.py:43
  1042.9 1.9 reduce.2
  1044.8 0.1 reshape.124
  1044.9 1.3 copy.18
  1046.2 66.1 %reduce-scatter.2.cloned.1.call-done = f32[128,384]{0,1:T(8,128)} async-done(((f32[128,6144]{0,1:T(8,128)}), f32[128,384]{0,1:T(8,128)}) %reduce-scatter.2.cloned.1.call-update) | async-done | bytes 196624 | tf_op jit(solution)/shard_map/reduce_scatter | solution.py:68
  1112.3 1.7 copy.19
Async XLA Ops:
  8.0 171.1 %copy-start = (bf16[192,384]{1,0:T(8,128)(2,1)S(1)}, bf16[192,384]{1,0:T(8,128)(2,1)}, u32[]{:S(2)}) copy-start(bf16[192,384]{1,0:T(8,128)(2,1)} %param.5) | copy-start | bytes 442372
  8.0 171.1 %all-gather.2.cloned.1.call-start = ((), (), s32[]{:S(2)}) async-start(), calls=%async_computation.7 | async-start | bytes 3244032 | tf_op jit(solution)/shard_map/all_gather | solution.py:55
  10.8 173.5 %all-to-all-start = ((bf16[32,1,12,512]{3,2,1,0:T(8,128)(2,1)}), bf16[32,1,12,512]{3,2,1,0:T(8,128)(2,1)}, u32[]{:S(2)}, u32[]{:S(2)}) async-start(bf16[32,1,12,512]{3,2,1,0:T(8,128)(2,1)} %bitcast.75), calls=%async_computation | async-start | bytes 1048576 | tf_op jit(solution)/shard_map/all_to_all | solution.py:51
  184.3 607.7 %all-to-all-start.2 = ((f32[32,128,192]{1,2,0:T(8,128)}), f32[32,128,192]{1,2,0:T(8,128)S(1)}, u32[]{:S(2)}, u32[]{:S(2)}) async-start(f32[32,128,192]{1,2,0:T(8,128)} %bitcast.77), calls=%async_computation.2 | async-start | bytes 6291456 | tf_op jit(solution)/shard_map/all_to_all | solution.py:60
  189.6 382.0 %all-reduce.4.cloned.1.call-start = ((), (), s32[]{:S(2)}) async-start(), calls=%async_computation.4 | async-start | bytes 2097152 | tf_op jit(solution)/shard_map/psum | solution.py:30
  364.8 416.7 %all-reduce.6.cloned.1.call-start = ((), (), s32[]{:S(2)}) async-start(), calls=%async_computation.5 | async-start | bytes 2097152 | tf_op jit(solution)/shard_map/psum | solution.py:30
  578.3 0.9 copy-start.3
  582.0 409.4 %all-reduce.8.cloned.1.call-start = ((), (), s32[]{:S(2)}) async-start(), calls=%async_computation.6 | async-start | bytes 2097152 | tf_op jit(solution)/shard_map/psum | solution.py:30
  788.2 0.9 copy-start.2
  791.9 320.3 %reduce-scatter.2.cloned.1.call-start = ((), (), s32[]{:S(2)}) async-start(), calls=%async_computation.8 | async-start | bytes 3342336 | tf_op jit(solution)/shard_map/reduce_scatter | solution.py:68
  792.0 1.6 copy-start.1
Sparse Core Ops, SparseCore 0:
  14.0 165.0 all-gather.1
Sparse Core Ops, SparseCore 1:
  364.9 206.6 all-reduce.3
  582.1 199.3 all-reduce.5
  792.0 199.4 all-reduce.7
  994.6 117.6 reduce-scatter.1
where the time goes:
time: 1130 us; the launch traced here: 1120 us
  waiting for transfers between devices  807 us (71%)
  blocking collectives  212 us (19%)
  matrix products  33.4 us (3%)
  starting transfers between devices  26.9 us (2%)
  local copies, waits for them, and re-layouts  19.9 us (2%)
  between operations  16.5 us (1%)
    psum x3, waiting for transfers between devices, owner_work(): gram = lax.psum(part, 'tensor')  593 us
    psum x1, blocking collectives, owner_work(): total = lax.psum(local_squares, 'tensor')  168 us
    all_gather x1, waiting for transfers between devices, body(): lax.all_gather(d_query, 'dp', axis=0, tiled=True)  147 us
    reduce_scatter x1, waiting for transfers between devices, body(): lax.psum_scatter(partial_sum, 'tensor', scatter_dimension=1, tiled=True)  66.1 us
    all_to_all x1, blocking collectives, owner_work(): lax.all_to_all(result[None], 'dp', split_axis=2, concat_axis=0, tiled=True)  43.9 us
  transfers between devices with their start and end apart: 7, of which 5 were waited for; matrix products, arithmetic and copies ran while one was open for 5% of the time, Pallas kernels for 0%

commit v1 on v0

v1 whole, which is shorter than its diff:
```python
import functools
import math

import jax
import jax.numpy as jnp
from jax import lax
from jax.experimental import pallas as pl
from jax.experimental.pallas import tpu as pltpu
from jax.sharding import Mesh, PartitionSpec as P

D = 6144
KV = 512
ITERS = 3
COEF_A = 3.4445
COEF_B = -4.775
COEF_C = 2.0315
BLK = 128
NB = KV // BLK
PAIRS = [(i, j) for i in range(NB) for j in range(i, NB)]
TINY = 2.0**-44
HALF_SCALE = 256.0

AXES = ("y", "x", "zh", "zl", "core")
COLUMN = ("zh", "zl", "core")
PLANE = ("y", "x")
F32 = jnp.float32
BF16 = jnp.bfloat16


def params(mib):
    return pltpu.CompilerParams(vmem_limit_bytes=mib << 20)


def gram_kernel(x_ref, o_ref):
    x = x_ref[...]
    gram = lax.dot_general(x, x, (((0,), (0,)), ((), ())), preferred_element_type=F32)
    for k, (i, j) in enumerate(PAIRS):
        o_ref[k * BLK : (k + 1) * BLK, :] = gram[i * BLK : (i + 1) * BLK, j * BLK : (j + 1) * BLK]


def gram_blocks(x):
    return pl.pallas_call(
        gram_kernel,
        out_shape=jax.ShapeDtypeStruct((len(PAIRS) * BLK, BLK), F32),
        compiler_params=params(16),
        cost_estimate=pl.CostEstimate(flops=2 * x.shape[0] * KV * KV, bytes_accessed=1 << 20, transcendentals=0),
        name="gram_blocks",
    )(x)


def sum_kernel(r_ref, o_ref):
    total = jnp.sum(r_ref[...], axis=0)
    for k in range(o_ref.shape[0]):
        o_ref[k] = total


def sum_and_repeat(r):
    return pl.pallas_call(
        sum_kernel,
        out_shape=jax.ShapeDtypeStruct(r.shape, F32),
        compiler_params=params(16),
        cost_estimate=pl.CostEstimate(flops=r.size, bytes_accessed=8 * r.size, transcendentals=0),
        name="sum_and_repeat",
    )(r)


def two(x):
    high = x.astype(BF16)
    return high, (x - high.astype(F32)).astype(BF16)


def mm(a, b):
    dot = functools.partial(jnp.dot, preferred_element_type=F32)
    return dot(a[0], b[0]) + (dot(a[0], b[1]) + dot(a[1], b[0]))


def newton_kernel(g_ref, x_ref, lift_ref, o_ref, m_ref):
    trace = jnp.zeros((1, 1), F32)
    for k, (i, j) in enumerate(PAIRS):
        block = g_ref[k * BLK : (k + 1) * BLK, :]
        m_ref[i * BLK : (i + 1) * BLK, j * BLK : (j + 1) * BLK] = block
        if i != j:
            m_ref[j * BLK : (j + 1) * BLK, i * BLK : (i + 1) * BLK] = block.T
        else:
            row = lax.broadcasted_iota(jnp.int32, (BLK, BLK), 0)
            col = lax.broadcasted_iota(jnp.int32, (BLK, BLK), 1)
            trace += jnp.sum(jnp.where(row == col, block, 0.0), keepdims=True)
    inverse = 1.0 / (jnp.sqrt(trace) + 1e-07)
    gram = m_ref[...] * inverse * inverse
    x = None
    for step in range(ITERS):
        parts = two(gram)
        rest = COEF_B * gram + COEF_C * mm(parts, parts)
        rest_parts = two(rest)
        if step + 1 < ITERS:
            half = COEF_A * gram + mm(parts, rest_parts)
            gram = COEF_A * half + mm(two(half), rest_parts)
        if step == 0:
            first = x_ref[...]
            dot = functools.partial(jnp.dot, preferred_element_type=F32)
            x = COEF_A * first.astype(F32) + (dot(first, rest_parts[0]) + dot(first, rest_parts[1]))
        else:
            x = COEF_A * x + mm(two(x), rest_parts)
    o_ref[...] = x * ((inverse * (math.sqrt(D) * HALF_SCALE)) * lift_ref[...])


def newton(g, x, lift):
    return pl.pallas_call(
        newton_kernel,
        out_shape=jax.ShapeDtypeStruct(x.shape, F32),
        scratch_shapes=[pltpu.VMEM((KV, KV), F32)],
        compiler_params=params(24),
        cost_estimate=pl.CostEstimate(flops=27 * 2 * KV**3, bytes_accessed=3 << 20, transcendentals=0),
        name="newton",
    )(g, x, lift)


def project_kernel(zh_ref, place_ref, q_ref, *refs):
    w_refs, (own_ref, other_ref) = refs[:-2], refs[-2:]
    zh = zh_ref[0]
    for ref, half in ((other_ref, 1 - zh), (own_ref, zh)):
        total = jnp.zeros(ref.shape, F32)
        for i, w_ref in enumerate(w_refs):
            for j in range(w_ref.shape[0]):
                q = q_ref[half, place_ref[i * w_ref.shape[0] + j]]
                total += lax.dot_general(q, w_ref[j], (((1,), (1,)), ((), ())), preferred_element_type=F32)
        ref[...] = total


def project(zh, place, q, ws):
    tokens, k = q.shape[2:]
    features = ws[0].shape[1]
    out = jax.ShapeDtypeStruct((tokens, features), F32)
    scalars = pl.BlockSpec(memory_space=pltpu.SMEM)
    return pl.pallas_call(
        project_kernel,
        in_specs=[scalars, scalars] + [pl.BlockSpec(memory_space=pltpu.VMEM)] * (1 + len(ws)),
        out_shape=[out, out],
        compiler_params=params(24),
        cost_estimate=pl.CostEstimate(flops=2 * q.size * features, bytes_accessed=6 << 20, transcendentals=0),
        name="project",
    )(zh, place, q, *ws)


def chunk_scale(rows):
    top = jnp.max(jnp.abs(rows.astype(F32)), axis=(1, 2), keepdims=True)
    return jnp.where((top < TINY) & (top > 0.0), TINY / jnp.maximum(top, 2.0**-126), 1.0)


def exchange(x, axes):
    return lax.all_to_all(x, axes, split_axis=0, concat_axis=0, tiled=True)


def round_ring(x, axis, steps):
    return [lax.ppermute(x, axis, [(i, (i + k) % 4) for i in range(4)]) for k in steps]


def turn(sizes):
    plane = sizes["y"] * sizes["x"]
    line = sizes["zl"] * sizes["core"]
    return [(p * line + t, (t ^ p) * line + p) for p in range(plane) for t in range(line)]


def body(sizes, grads, d_query, w_query):
    mats, own_rows, kv = grads.shape
    packed = (mats, own_rows * kv // BLK, BLK)
    zh = lax.axis_index("zh")
    turned = lax.ppermute(w_query, ("y", "x", "zl", "core"), turn(sizes))
    steps_y, steps_x = jnp.arange(sizes["y"])[:, None], jnp.arange(sizes["x"])[None, :]
    from_y = (lax.axis_index("y") - steps_y) % sizes["y"]
    from_x = (lax.axis_index("x") - steps_x) % sizes["x"]
    own_line = lax.axis_index(("zl", "core"))
    place = ((from_y * sizes["x"] + from_x) ^ own_line).reshape(-1).astype(jnp.int32)

    received = exchange(grads.reshape(packed), COLUMN)
    received, turned = lax.optimization_barrier((received, turned))
    rows = received.reshape(mats * own_rows, kv)
    later_query, _ = lax.optimization_barrier((d_query, received))
    queries = lax.all_gather(later_query, COLUMN, axis=0, tiled=True)
    blocks = gram_blocks(rows)
    plane = sizes["y"] * sizes["x"]
    partial, along_x = lax.optimization_barrier(
        (exchange(blocks.reshape(plane, -1, BLK), PLANE), round_ring(turned, "x", (1, 2, 3)))
    )
    along_x = jnp.stack([turned] + along_x)
    lift = jnp.repeat(chunk_scale(received).reshape(mats, 1), own_rows, axis=0)
    gram, lift = lax.optimization_barrier((exchange(sum_and_repeat(partial), PLANE).reshape(-1, BLK), lift))
    result, behind, ahead = lax.optimization_barrier((newton(gram, rows, lift), *round_ring(along_x, "y", (1, 3))))
    (opposite,) = round_ring(behind, "y", (1,))
    weights = [along_x, behind, opposite, ahead]
    sent = result.astype(jnp.float16).reshape(packed)
    returned = exchange(sent, COLUMN)

    tokens, heads = d_query.shape
    line = sizes["zl"] * sizes["core"]
    own, other = project(
        zh.reshape(1).astype(jnp.int32),
        place,
        queries.reshape(sizes["zh"], line, tokens, heads),
        weights,
    )
    returned, swapped = lax.optimization_barrier((returned, lax.ppermute(other, "zh", [(0, 1), (1, 0)])))
    updates = returned.reshape(grads.shape).astype(F32) * (1.0 / (HALF_SCALE * chunk_scale(grads)))
    first = zh == 0
    d_input = jnp.concatenate([jnp.where(first, own, swapped), jnp.where(first, swapped, own)], axis=1)
    return updates, d_input


def solution(mesh):
    sizes = dict(zip(AXES, (4, 4, 2, 8, 2)))
    fine = Mesh(mesh.devices.reshape(tuple(sizes.values())), AXES)
    rows = P(None, ("zl", "core", "y", "x", "zh"), None)
    flat = P(("y", "x", "zh"), ("zl", "core"))
    return jax.shard_map(
        functools.partial(body, sizes),
        mesh=fine,
        in_specs=(rows, flat, flat),
        out_specs=(rows, flat),
        check_vma=False,
    )
```

time: 1130 us -> 190 us (0.17)
  the two profiles are of different devices: /device:TPU:1 before, /device:TPU:32 now
where the time goes in v1:
time: 190 us; the launch traced here: 189 us
  waiting for transfers between devices  76.2 us (40%)
  starting transfers between devices  75.5 us (40%)
  between operations  14.3 us (8%)
  Pallas kernels  12.9 us (7%)
  local copies, waits for them, and re-layouts  7.23 us (4%)
  other arithmetic  2.71 us (1%)
    all_to_all x4, starting transfers between devices, exchange(): return lax.all_to_all(x, axes, split_axis=0, concat_axis=0, tiled=True)  38.3 us
    ppermute x1, waiting for transfers between devices, body(): turned = lax.ppermute(w_query, ('y', 'x', 'zl', 'core'), turn(sizes))  35.1 us
    ppermute x6, starting transfers between devices, round_ring(): lax.ppermute(x, axis, [(i, (i + k) % 4) for i in range(4)])  21.3 us
    ppermute x6, waiting for transfers between devices, round_ring(): lax.ppermute(x, axis, [(i, (i + k) % 4) for i in range(4)])  19.2 us
    ppermute x1, waiting for transfers between devices, body(): lax.ppermute(other, 'zh', [(0, 1), (1, 0)])  12 us
    ppermute x1, starting transfers between devices, body(): lax.ppermute(other, 'zh', [(0, 1), (1, 0)])  11.2 us
    all_to_all x4, waiting for transfers between devices, exchange(): return lax.all_to_all(x, axes, split_axis=0, concat_axis=0, tiled=True)  9.86 us
    pallas_call x1, Pallas kernels, newton(): pl.pallas_call(newton_kernel, out_shape=jax.ShapeDtypeStruct(x.shape, F32...  8.15 us
  transfers between devices with their start and end apart: 13, of which 7 were waited for; matrix products, arithmetic and copies ran while one was open for 1% of the time, Pallas kernels for 7%

profile of v1, /device:TPU:32, one launch (start us, length us, event | category | flops | bytes accessed | tf_op | source)
XLA Modules:
  0.0 188.7 jit_solution(2546121332527208880)
XLA Ops:
  7.2 1.2 copy.5
  8.4 1.0 reshape.112
  9.4 15.4 %all-to-all-start = ((bf16[32,48,128]{2,1,0:T(8,128)(2,1)}), bf16[32,48,128]{2,1,0:T(8,128)(2,1)S(1)}, u32[]{:S(2)}, u32[]{:S(2)}) async-start(bf16[32,48,128]{2,1,0:T(8,128)(2,1)} %reshape.112), calls=%async_computation | async-start | bytes 786432 | tf_op jit(solution)/shard_map/all_to_all | solution.py:151
  24.7 0.0 all-gather.2.cloned.1.call-start
  24.8 4.6 %collective-permute-start = (bf16[192,384]{1,0:T(8,128)(2,1)}, bf16[192,384]{1,0:T(8,128)(2,1)S(1)}, u32[]{:S(2)}, u32[]{:S(2)}) collective-permute-start(bf16[192,384]{1,0:T(8,128)(2,1)} %param.5), channel_id=1, source_target_pairs={{0,0},{1,32},{2,64},{3,96},{4,128},{5,160},{6,192},{7,224},{8,256}... | collective-permute-start | bytes 442376 | tf_op jit(solution)/shard_map/ppermute | solution.py:168
  29.4 35.1 %collective-permute-done = bf16[192,384]{1,0:T(8,128)(2,1)S(1)} collective-permute-done((bf16[192,384]{1,0:T(8,128)(2,1)}, bf16[192,384]{1,0:T(8,128)(2,1)S(1)}, u32[]{:S(2)}, u32[]{:S(2)}) %collective-permute-start) | collective-permute-done | bytes 147488 | tf_op jit(solution)/shard_map/ppermute | solution.py:168
  64.5 6.7 %all-to-all-done = bf16[32,48,128]{2,1,0:T(8,128)(2,1)S(1)} async-done(((bf16[32,48,128]{2,1,0:T(8,128)(2,1)}), bf16[32,48,128]{2,1,0:T(8,128)(2,1)S(1)}, u32[]{:S(2)}, u32[]{:S(2)}) %all-to-all-start) | async-done | bytes 393248 | tf_op jit(solution)/shard_map/all_to_all | solution.py:151
  71.2 0.0 all-gather.2.cloned.1.call-update
  71.2 0.2 reshape.113.x_ref
  71.4 1.3 gram_blocks.1
  72.7 3.6 %all-to-all-start.1 = ((f32[16,80,128]{2,1,0:T(8,128)}), f32[16,80,128]{2,1,0:T(8,128)S(1)}, u32[]{:S(2)}, u32[]{:S(2)}) async-start(f32[16,80,128]{2,1,0:T(8,128)} %bitcast), calls=%async_computation.1 | async-start | bytes 1310720 | tf_op jit(solution)/shard_map/all_to_all | solution.py:151
  76.3 3.7 %collective-permute-start.1 = (bf16[192,384]{1,0:T(8,128)(2,1)S(1)}, bf16[192,384]{1,0:T(8,128)(2,1)S(1)}, u32[]{:S(2)}, u32[]{:S(2)}) collective-permute-start(bf16[192,384]{1,0:T(8,128)(2,1)S(1)} %collective-permute-done), channel_id=1, source_target_pairs={{0,32},{32,64},{64,96},{96,0},{1,33},{33,65},{65,97},{97,1},{2,34}... | collective-permute-start | bytes 442376 | tf_op jit(solution)/shard_map/ppermute | solution.py:155
  80.1 4.6 %collective-permute-start.2 = (bf16[192,384]{1,0:T(8,128)(2,1)S(1)}, bf16[192,384]{1,0:T(8,128)(2,1)S(1)}, u32[]{:S(2)}, u32[]{:S(2)}) collective-permute-start(bf16[192,384]{1,0:T(8,128)(2,1)S(1)} %collective-permute-done), channel_id=1, source_target_pairs={{0,64},{32,96},{64,0},{96,32},{1,65},{33,97},{65,1},{97,33},{2,66}... | collective-permute-start | bytes 442376 | tf_op jit(solution)/shard_map/ppermute | solution.py:155
  84.7 3.4 %collective-permute-start.3 = (bf16[192,384]{1,0:T(8,128)(2,1)S(1)}, bf16[192,384]{1,0:T(8,128)(2,1)S(1)}, u32[]{:S(2)}, u32[]{:S(2)}) collective-permute-start(bf16[192,384]{1,0:T(8,128)(2,1)S(1)} %collective-permute-done), channel_id=1, source_target_pairs={{0,96},{32,0},{64,32},{96,64},{1,97},{33,1},{65,33},{97,65},{2,98}... | collective-permute-start | bytes 442376 | tf_op jit(solution)/shard_map/ppermute | solution.py:155
  88.0 0.0 collective-permute-done.1
  88.0 0.6 collective-permute-done.2
  88.6 3.1 %collective-permute-done.3 = bf16[192,384]{1,0:T(8,128)(2,1)S(1)} collective-permute-done((bf16[192,384]{1,0:T(8,128)(2,1)S(1)}, bf16[192,384]{1,0:T(8,128)(2,1)S(1)}, u32[]{:S(2)}, u32[]{:S(2)}) %collective-permute-start.3) | collective-permute-done | bytes 147488 | tf_op jit(solution)/shard_map/ppermute | solution.py:155
  91.7 0.0 all-to-all-done.1.r_ref
  91.7 0.9 sum_and_repeat.1
  92.6 6.5 %all-to-all-start.2 = ((f32[16,80,128]{2,1,0:T(8,128)}), f32[16,80,128]{2,1,0:T(8,128)S(1)}, u32[]{:S(2)}, u32[]{:S(2)}) async-start(f32[16,80,128]{2,1,0:T(8,128)} %sum_and_repeat.1), calls=%async_computation.2 | async-start | bytes 1310720 | tf_op jit(solution)/shard_map/all_to_all | solution.py:151
  99.1 0.3 abs_reduce_fusion.1
  99.4 0.1 broadcast_in_dim.15
  99.5 0.1 broadcast_in_dim.16
  99.6 0.1 pad_maximum_fusion.refs_0_
  99.7 3.8 %collective-permute-start.4 = (bf16[4,192,384]{2,1,0:T(8,128)(2,1)S(1)}, bf16[4,192,384]{2,1,0:T(8,128)(2,1)S(1)}, u32[]{:S(2)}, u32[]{:S(2)}) collective-permute-start(bf16[4,192,384]{2,1,0:T(8,128)(2,1)S(1)} %pad_maximum_fusion.refs_0_), channel_id=1, source_target_pairs={{0,128},{128,256},{256,384},{384,0},{1,129},{129,257},{257,385},{3... | collective-permute-start | bytes 1769480 | tf_op jit(solution)/shard_map/ppermute | solution.py:155
  103.6 3.2 %collective-permute-start.5 = (bf16[4,192,384]{2,1,0:T(8,128)(2,1)S(1)}, bf16[4,192,384]{2,1,0:T(8,128)(2,1)S(1)}, u32[]{:S(2)}, u32[]{:S(2)}) collective-permute-start(bf16[4,192,384]{2,1,0:T(8,128)(2,1)S(1)} %pad_maximum_fusion.refs_0_), channel_id=1, source_target_pairs={{0,384},{128,0},{256,128},{384,256},{1,385},{129,1},{257,129},{385... | collective-permute-start | bytes 1769480 | tf_op jit(solution)/shard_map/ppermute | solution.py:155
  106.8 3.2 %all-to-all-done.2 = f32[16,80,128]{2,1,0:T(8,128)S(1)} async-done(((f32[16,80,128]{2,1,0:T(8,128)}), f32[16,80,128]{2,1,0:T(8,128)S(1)}, u32[]{:S(2)}, u32[]{:S(2)}) %all-to-all-start.2) | async-done | bytes 655392 | tf_op jit(solution)/shard_map/all_to_all | solution.py:151
  110.0 0.1 copy.6.lift_ref
  110.1 0.0 copy-start.1
  110.1 8.1 %newton.1 = f32[384,512]{1,0:T(8,128)S(1)} custom-call(f32[1280,128]{1,0:T(8,128)S(1)} %bitcast.9, bf16[384,512]{1,0:T(8,128)(2,1)S(1)} %reshape.113.x_ref, f32[384,1]{1,0:T(8,128)S(1)} %copy.6.lift_ref), custom_call_target="tpu_custom_call" | custom-call | flops 7247757312 | bytes 3145728 | tf_op jit(solution)/shard_map/newton/pallas_call | solution.py:108
  118.3 0.0 collective-permute-done.4.refs_1_
  118.3 0.0 collective-permute-done.5.refs_3_
  118.3 0.1 convert_element_type.16
  118.4 1.0 reshape.116
  119.4 12.9 %all-to-all-start.3 = ((f16[32,48,128]{2,1,0:T(8,128)(2,1)}), f16[32,48,128]{2,1,0:T(8,128)(2,1)}, u32[]{:S(2)}, u32[]{:S(2)}) async-start(f16[32,48,128]{2,1,0:T(8,128)(2,1)} %reshape.116), calls=%async_computation.3 | async-start | bytes 786432 | tf_op jit(solution)/shard_map/all_to_all | solution.py:151
  132.3 2.6 %collective-permute-start.6 = (bf16[4,192,384]{2,1,0:T(8,128)(2,1)S(1)}, bf16[4,192,384]{2,1,0:T(8,128)(2,1)S(1)}, u32[]{:S(2)}, u32[]{:S(2)}) collective-permute-start(bf16[4,192,384]{2,1,0:T(8,128)(2,1)S(1)} %collective-permute-done.4.refs_1_), channel_id=1, source_target_pairs={{0,128},{128,256},{256,384},{384,0},{1,129},{129,257},{257,385},{3... | collective-permute-start | bytes 1769480 | tf_op jit(solution)/shard_map/ppermute | solution.py:155
  134.9 0.1 add_xor_fusion
  135.0 0.1 xor.12.place_ref
  135.1 0.0 copy-done.1
  135.1 0.1 abs_reduce_fusion
  135.2 15.6 %collective-permute-done.6.refs_2_ = bf16[4,192,384]{2,1,0:T(8,128)(2,1)S(1)} collective-permute-done((bf16[4,192,384]{2,1,0:T(8,128)(2,1)S(1)}, bf16[4,192,384]{2,1,0:T(8,128)(2,1)S(1)}, u32[]{:S(2)}, u32[]{:S(2)}) %collective-permute-start.6) | collective-permute-done | bytes 589856 | tf_op jit(solution)/shard_map/ppermute | solution.py:155
  150.8 0.0 all-gather.2.cloned.1.call-done
  150.8 0.0 copy-start
  150.8 1.9 %copy-done = bf16[4096,384]{1,0:T(8,128)(2,1)S(1)} copy-done((bf16[4096,384]{1,0:T(8,128)(2,1)S(1)}, bf16[4096,384]{1,0:T(8,128)(2,1)}, u32[]{:S(2)}) %copy-start) | copy-done | bytes 3145752
  152.7 2.6 %project.1 = (f32[128,192]{1,0:T(8,128)S(1)}, f32[128,192]{1,0:T(8,128)S(1)}) custom-call(s32[1]{0:T(128)} %bitcast.6.zh_ref, s32[16]{0:T(128)S(1)} %xor.12.place_ref, bf16[2,16,128,384]{3,2,1,0:T(8,128)(2,1)S(1)} %bitcast.8, bf16[4,192,384]{2,1,0:T(8,128)(2,1)S(1)} %pad_maximum_fusion.refs_0_, bf16[4,192,384]{2,1,0:T(8,128)(2,1)S(1)} %collective-permute-done.4.refs_1_, ...), custom_call_target="tpu_custom_call" | custom-call | flops 603979776 | bytes 6291456 | tf_op jit(solution)/shard_map/project/pallas_call | solution.py:135
  155.2 11.2 %collective-permute-start.7 = (f32[128,192]{1,0:T(8,128)S(1)}, f32[128,192]{1,0:T(8,128)S(1)}, u32[]{:S(2)}, u32[]{:S(2)}) collective-permute-start(f32[128,192]{1,0:T(8,128)S(1)} %get-tuple-element.30), channel_id=1, source_target_pairs={{0,16},{16,0},{1,17},{17,1},{2,18},{18,2},{3,19},{19,3},{4,20},{20... | collective-permute-start | bytes 294920 | tf_op jit(solution)/shard_map/ppermute | solution.py:202
  166.5 0.0 all-to-all-done.3
  166.5 12.0 %collective-permute-done.7 = f32[128,192]{1,0:T(8,128)S(1)} collective-permute-done((f32[128,192]{1,0:T(8,128)S(1)}, f32[128,192]{1,0:T(8,128)S(1)}, u32[]{:S(2)}, u32[]{:S(2)}) %collective-permute-start.7) | collective-permute-done | bytes 98336 | tf_op jit(solution)/shard_map/ppermute | solution.py:202
  178.4 1.0 convert_element_type.20
  179.5 0.1 reshape.119
  179.6 0.1 broadcast_multiply_fusion
  179.8 1.3 copy.7
  181.1 0.8 pad_maximum_fusion.1
  (4 shorter events, 0.1 us)
Async XLA Ops:
  9.4 61.8 %all-to-all-start = ((bf16[32,48,128]{2,1,0:T(8,128)(2,1)}), bf16[32,48,128]{2,1,0:T(8,128)(2,1)S(1)}, u32[]{:S(2)}, u32[]{:S(2)}) async-start(bf16[32,48,128]{2,1,0:T(8,128)(2,1)} %reshape.112), calls=%async_computation | async-start | bytes 786432 | tf_op jit(solution)/shard_map/all_to_all | solution.py:151
  24.7 126.0 %all-gather.2.cloned.1.call-start = ((), (), s32[]{:S(2)}) async-start(), calls=%async_computation.4 | async-start | bytes 3244032 | tf_op jit(solution)/shard_map/all_gather | solution.py:179
  24.8 39.7 %collective-permute-start = (bf16[192,384]{1,0:T(8,128)(2,1)}, bf16[192,384]{1,0:T(8,128)(2,1)S(1)}, u32[]{:S(2)}, u32[]{:S(2)}) collective-permute-start(bf16[192,384]{1,0:T(8,128)(2,1)} %param.5), channel_id=1, source_target_pairs={{0,0},{1,32},{2,64},{3,96},{4,128},{5,160},{6,192},{7,224},{8,256}... | collective-permute-start | bytes 442376 | tf_op jit(solution)/shard_map/ppermute | solution.py:168
  72.7 19.0 %all-to-all-start.1 = ((f32[16,80,128]{2,1,0:T(8,128)}), f32[16,80,128]{2,1,0:T(8,128)S(1)}, u32[]{:S(2)}, u32[]{:S(2)}) async-start(f32[16,80,128]{2,1,0:T(8,128)} %bitcast), calls=%async_computation.1 | async-start | bytes 1310720 | tf_op jit(solution)/shard_map/all_to_all | solution.py:151
  76.3 11.7 %collective-permute-start.1 = (bf16[192,384]{1,0:T(8,128)(2,1)S(1)}, bf16[192,384]{1,0:T(8,128)(2,1)S(1)}, u32[]{:S(2)}, u32[]{:S(2)}) collective-permute-start(bf16[192,384]{1,0:T(8,128)(2,1)S(1)} %collective-permute-done), channel_id=1, source_target_pairs={{0,32},{32,64},{64,96},{96,0},{1,33},{33,65},{65,97},{97,1},{2,34}... | collective-permute-start | bytes 442376 | tf_op jit(solution)/shard_map/ppermute | solution.py:155
  80.1 8.5 %collective-permute-start.2 = (bf16[192,384]{1,0:T(8,128)(2,1)S(1)}, bf16[192,384]{1,0:T(8,128)(2,1)S(1)}, u32[]{:S(2)}, u32[]{:S(2)}) collective-permute-start(bf16[192,384]{1,0:T(8,128)(2,1)S(1)} %collective-permute-done), channel_id=1, source_target_pairs={{0,64},{32,96},{64,0},{96,32},{1,65},{33,97},{65,1},{97,33},{2,66}... | collective-permute-start | bytes 442376 | tf_op jit(solution)/shard_map/ppermute | solution.py:155
  84.7 7.0 %collective-permute-start.3 = (bf16[192,384]{1,0:T(8,128)(2,1)S(1)}, bf16[192,384]{1,0:T(8,128)(2,1)S(1)}, u32[]{:S(2)}, u32[]{:S(2)}) collective-permute-start(bf16[192,384]{1,0:T(8,128)(2,1)S(1)} %collective-permute-done), channel_id=1, source_target_pairs={{0,96},{32,0},{64,32},{96,64},{1,97},{33,1},{65,33},{97,65},{2,98}... | collective-permute-start | bytes 442376 | tf_op jit(solution)/shard_map/ppermute | solution.py:155
  92.6 17.4 %all-to-all-start.2 = ((f32[16,80,128]{2,1,0:T(8,128)}), f32[16,80,128]{2,1,0:T(8,128)S(1)}, u32[]{:S(2)}, u32[]{:S(2)}) async-start(f32[16,80,128]{2,1,0:T(8,128)} %sum_and_repeat.1), calls=%async_computation.2 | async-start | bytes 1310720 | tf_op jit(solution)/shard_map/all_to_all | solution.py:151
  99.7 18.6 %collective-permute-start.4 = (bf16[4,192,384]{2,1,0:T(8,128)(2,1)S(1)}, bf16[4,192,384]{2,1,0:T(8,128)(2,1)S(1)}, u32[]{:S(2)}, u32[]{:S(2)}) collective-permute-start(bf16[4,192,384]{2,1,0:T(8,128)(2,1)S(1)} %pad_maximum_fusion.refs_0_), channel_id=1, source_target_pairs={{0,128},{128,256},{256,384},{384,0},{1,129},{129,257},{257,385},{3... | collective-permute-start | bytes 1769480 | tf_op jit(solution)/shard_map/ppermute | solution.py:155
  103.6 14.7 %collective-permute-start.5 = (bf16[4,192,384]{2,1,0:T(8,128)(2,1)S(1)}, bf16[4,192,384]{2,1,0:T(8,128)(2,1)S(1)}, u32[]{:S(2)}, u32[]{:S(2)}) collective-permute-start(bf16[4,192,384]{2,1,0:T(8,128)(2,1)S(1)} %pad_maximum_fusion.refs_0_), channel_id=1, source_target_pairs={{0,384},{128,0},{256,128},{384,256},{1,385},{129,1},{257,129},{385... | collective-permute-start | bytes 1769480 | tf_op jit(solution)/shard_map/ppermute | solution.py:155
  110.1 24.9 %copy-start.1 = (bf16[32,12,512]{2,0,1:T(8,128)(2,1)S(1)}, bf16[32,12,512]{2,0,1:T(8,128)(2,1)}, u32[]{:S(2)}) copy-start(bf16[32,12,512]{2,0,1:T(8,128)(2,1)} %param.3) | copy-start | bytes 1179652
  119.4 47.1 %all-to-all-start.3 = ((f16[32,48,128]{2,1,0:T(8,128)(2,1)}), f16[32,48,128]{2,1,0:T(8,128)(2,1)}, u32[]{:S(2)}, u32[]{:S(2)}) async-start(f16[32,48,128]{2,1,0:T(8,128)(2,1)} %reshape.116), calls=%async_computation.3 | async-start | bytes 786432 | tf_op jit(solution)/shard_map/all_to_all | solution.py:151
  132.3 18.5 %collective-permute-start.6 = (bf16[4,192,384]{2,1,0:T(8,128)(2,1)S(1)}, bf16[4,192,384]{2,1,0:T(8,128)(2,1)S(1)}, u32[]{:S(2)}, u32[]{:S(2)}) collective-permute-start(bf16[4,192,384]{2,1,0:T(8,128)(2,1)S(1)} %collective-permute-done.4.refs_1_), channel_id=1, source_target_pairs={{0,128},{128,256},{256,384},{384,0},{1,129},{129,257},{257,385},{3... | collective-permute-start | bytes 1769480 | tf_op jit(solution)/shard_map/ppermute | solution.py:155
  150.8 1.9 %copy-start = (bf16[4096,384]{1,0:T(8,128)(2,1)S(1)}, bf16[4096,384]{1,0:T(8,128)(2,1)}, u32[]{:S(2)}) copy-start(bf16[4096,384]{1,0:T(8,128)(2,1)} %all-gather.2.cloned.1.call-done) | copy-start | bytes 9437188
  155.2 23.2 %collective-permute-start.7 = (f32[128,192]{1,0:T(8,128)S(1)}, f32[128,192]{1,0:T(8,128)S(1)}, u32[]{:S(2)}, u32[]{:S(2)}) collective-permute-start(f32[128,192]{1,0:T(8,128)S(1)} %get-tuple-element.30), channel_id=1, source_target_pairs={{0,16},{16,0},{1,17},{17,1},{2,18},{18,2},{3,19},{19,3},{4,20},{20... | collective-permute-start | bytes 294920 | tf_op jit(solution)/shard_map/ppermute | solution.py:202
Sparse Core Ops, SparseCore 0:
  71.3 66.1 all-gather.1

commit v2 on v1

--- a/solution.py
+++ b/solution.py
@@ -59,9 +59,23 @@
         sum_kernel,
         out_shape=jax.ShapeDtypeStruct(r.shape, F32),
         compiler_params=params(16),
-        cost_estimate=pl.CostEstimate(flops=r.size, bytes_accessed=8 * r.size, transcendentals=0),
+        cost_estimate=pl.CostEstimate(flops=5 * 10**9, bytes_accessed=8 * r.size, transcendentals=0),
         name="sum_and_repeat",
     )(r)
+
+
+def relay_kernel(x_ref, o_ref):
+    o_ref[...] = x_ref[...]
+
+
+def relay(x):
+    return pl.pallas_call(
+        relay_kernel,
+        out_shape=jax.ShapeDtypeStruct(x.shape, x.dtype),
+        compiler_params=params(16),
+        cost_estimate=pl.CostEstimate(flops=5 * 10**10, bytes_accessed=4 * x.size, transcendentals=0),
+        name="relay",
+    )(x)
 
 
 def two(x):
@@ -137,7 +151,7 @@
         in_specs=[scalars, scalars] + [pl.BlockSpec(memory_space=pltpu.VMEM)] * (1 + len(ws)),
         out_shape=[out, out],
         compiler_params=params(24),
-        cost_estimate=pl.CostEstimate(flops=2 * q.size * features, bytes_accessed=6 << 20, transcendentals=0),
+        cost_estimate=pl.CostEstimate(flops=10**12, bytes_accessed=6 << 20, transcendentals=0),
         name="project",
     )(zh, place, q, *ws)
 
@@ -155,10 +169,14 @@
     return [lax.ppermute(x, axis, [(i, (i + k) % 4) for i in range(4)]) for k in steps]
 
 
+def spread(p):
+    return ((p << 1) & 15) ^ ((p >> 3) * 3)
+
+
 def turn(sizes):
     plane = sizes["y"] * sizes["x"]
     line = sizes["zl"] * sizes["core"]
-    return [(p * line + t, (t ^ p) * line + p) for p in range(plane) for t in range(line)]
+    return [(p * line + t, (t ^ spread(p)) * line + p) for p in range(plane) for t in range(line)]
 
 
 def body(sizes, grads, d_query, w_query):
@@ -170,22 +188,24 @@
     from_y = (lax.axis_index("y") - steps_y) % sizes["y"]
     from_x = (lax.axis_index("x") - steps_x) % sizes["x"]
     own_line = lax.axis_index(("zl", "core"))
-    place = ((from_y * sizes["x"] + from_x) ^ own_line).reshape(-1).astype(jnp.int32)
-
-    received = exchange(grads.reshape(packed), COLUMN)
-    received, turned = lax.optimization_barrier((received, turned))
+    place = ((from_y * sizes["x"] + from_x) ^ spread(own_line)).reshape(-1).astype(jnp.int32)
+
+    turned = relay(turned)
+    received, along_x = lax.optimization_barrier(
+        (exchange(grads.reshape(packed), COLUMN), round_ring(turned, "x", (1, 2, 3)))
+    )
+    along_x = jnp.stack([turned] + along_x)
     rows = received.reshape(mats * own_rows, kv)
-    later_query, _ = lax.optimization_barrier((d_query, received))
+    later_query, _ = lax.optimization_barrier((d_query, w_query))
     queries = lax.all_gather(later_query, COLUMN, axis=0, tiled=True)
     blocks = gram_blocks(rows)
     plane = sizes["y"] * sizes["x"]
-    partial, along_x = lax.optimization_barrier(
-        (exchange(blocks.reshape(plane, -1, BLK), PLANE), round_ring(turned, "x", (1, 2, 3)))
-    )
-    along_x = jnp.stack([turned] + along_x)
+    partial = exchange(blocks.reshape(plane, -1, BLK), PLANE)
     lift = jnp.repeat(chunk_scale(received).reshape(mats, 1), own_rows, axis=0)
-    gram, lift = lax.optimization_barrier((exchange(sum_and_repeat(partial), PLANE).reshape(-1, BLK), lift))
-    result, behind, ahead = lax.optimization_barrier((newton(gram, rows, lift), *round_ring(along_x, "y", (1, 3))))
+    gram, behind, ahead, lift = lax.optimization_barrier(
+        (exchange(sum_and_repeat(partial), PLANE).reshape(-1, BLK), *round_ring(along_x, "y", (1, 3)), lift)
+    )
+    result = newton(gram, rows, lift)
     (opposite,) = round_ring(behind, "y", (1,))
     weights = [along_x, behind, opposite, ahead]
     sent = result.astype(jnp.float16).reshape(packed)

time: 190 us -> 173 us (0.911)
  the two profiles are of different devices: /device:TPU:32 before, /device:TPU:1 now
where the time goes in v2:
time: 173 us
  starting transfers between devices  74.8 us (43%)
  waiting for transfers between devices  58.5 us (34%)
  between operations  14.3 us (8%)
  Pallas kernels  13.5 us (8%)
  local copies, waits for them, and re-layouts  7.22 us (4%)
  other arithmetic  4.23 us (2%)
    all_to_all x4, starting transfers between devices, exchange(): return lax.all_to_all(x, axes, split_axis=0, concat_axis=0, tiled=True)  40.3 us
    all_to_all x4, waiting for transfers between devices, exchange(): return lax.all_to_all(x, axes, split_axis=0, concat_axis=0, tiled=True)  33.1 us
    ppermute x6, starting transfers between devices, round_ring(): lax.ppermute(x, axis, [(i, (i + k) % 4) for i in range(4)])  17.9 us
    ppermute x6, waiting for transfers between devices, round_ring(): lax.ppermute(x, axis, [(i, (i + k) % 4) for i in range(4)])  12 us
    ppermute x1, starting transfers between devices, body(): lax.ppermute(other, 'zh', [(0, 1), (1, 0)])  12 us
    ppermute x1, waiting for transfers between devices, body(): lax.ppermute(other, 'zh', [(0, 1), (1, 0)])  11.1 us
    pallas_call x1, Pallas kernels, newton(): pl.pallas_call(newton_kernel, out_shape=jax.ShapeDtypeStruct(x.shape, F32...  8.15 us
    ppermute x1, starting transfers between devices, body(): turned = lax.ppermute(w_query, ('y', 'x', 'zl', 'core'), turn(sizes))  4.51 us
  transfers between devices with their start and end apart: 13, of which 10 were waited for; matrix products, arithmetic and copies ran while one was open for 4% of the time, Pallas kernels for 8%

profile of v2, /device:TPU:1, one launch (start us, length us, event | category | flops | bytes accessed | tf_op | source)
XLA Modules:
  0.0 172.5 jit_solution(2043505814013678013)
XLA Ops:
  7.2 4.5 %collective-permute-start = (bf16[192,384]{1,0:T(8,128)(2,1)}, bf16[192,384]{1,0:T(8,128)(2,1)S(1)}, u32[]{:S(2)}, u32[]{:S(2)}) collective-permute-start(bf16[192,384]{1,0:T(8,128)(2,1)} %param.5), channel_id=1, source_target_pairs={{0,0},{1,32},{2,64},{3,96},{4,128},{5,160},{6,192},{7,224},{8,256}... | collective-permute-start | bytes 442376 | tf_op jit(solution)/shard_map/ppermute | solution.py:186
  11.7 1.2 copy.5
  12.9 1.0 reshape.112
  13.9 19.8 %all-to-all-start = ((bf16[32,48,128]{2,1,0:T(8,128)(2,1)}), bf16[32,48,128]{2,1,0:T(8,128)(2,1)S(1)}, u32[]{:S(2)}, u32[]{:S(2)}) async-start(bf16[32,48,128]{2,1,0:T(8,128)(2,1)} %reshape.112), calls=%async_computation | async-start | bytes 786432 | tf_op jit(solution)/shard_map/all_to_all | solution.py:165
  33.7 0.0 all-gather.2.cloned.1.call-start
  33.8 0.7 all-gather.2.cloned.1.call-update
  34.4 1.6 collective-permute-done.x_ref
  36.0 1.9 %collective-permute-start.1 = (bf16[192,384]{1,0:T(8,128)(2,1)S(1)}, bf16[192,384]{1,0:T(8,128)(2,1)S(1)}, u32[]{:S(2)}, u32[]{:S(2)}) collective-permute-start(bf16[192,384]{1,0:T(8,128)(2,1)S(1)} %relay.1), channel_id=1, source_target_pairs={{0,32},{32,64},{64,96},{96,0},{1,33},{33,65},{65,97},{97,1},{2,34}... | collective-permute-start | bytes 442376 | tf_op jit(solution)/shard_map/ppermute | solution.py:169
  38.0 1.9 %collective-permute-start.2 = (bf16[192,384]{1,0:T(8,128)(2,1)S(1)}, bf16[192,384]{1,0:T(8,128)(2,1)S(1)}, u32[]{:S(2)}, u32[]{:S(2)}) collective-permute-start(bf16[192,384]{1,0:T(8,128)(2,1)S(1)} %relay.1), channel_id=1, source_target_pairs={{0,64},{32,96},{64,0},{96,32},{1,65},{33,97},{65,1},{97,33},{2,66}... | collective-permute-start | bytes 442376 | tf_op jit(solution)/shard_map/ppermute | solution.py:169
  39.9 4.6 %collective-permute-start.3 = (bf16[192,384]{1,0:T(8,128)(2,1)S(1)}, bf16[192,384]{1,0:T(8,128)(2,1)S(1)}, u32[]{:S(2)}, u32[]{:S(2)}) collective-permute-start(bf16[192,384]{1,0:T(8,128)(2,1)S(1)} %relay.1), channel_id=1, source_target_pairs={{0,96},{32,0},{64,32},{96,64},{1,97},{33,1},{65,33},{97,65},{2,98}... | collective-permute-start | bytes 442376 | tf_op jit(solution)/shard_map/ppermute | solution.py:169
  44.5 0.0 collective-permute-done.1
  44.5 1.2 collective-permute-done.2
  45.7 2.2 %collective-permute-done.3 = bf16[192,384]{1,0:T(8,128)(2,1)S(1)} collective-permute-done((bf16[192,384]{1,0:T(8,128)(2,1)S(1)}, bf16[192,384]{1,0:T(8,128)(2,1)S(1)}, u32[]{:S(2)}, u32[]{:S(2)}) %collective-permute-start.3) | collective-permute-done | bytes 147488 | tf_op jit(solution)/shard_map/ppermute | solution.py:169
  47.9 13.8 %all-to-all-done = bf16[32,48,128]{2,1,0:T(8,128)(2,1)S(1)} async-done(((bf16[32,48,128]{2,1,0:T(8,128)(2,1)}), bf16[32,48,128]{2,1,0:T(8,128)(2,1)S(1)}, u32[]{:S(2)}, u32[]{:S(2)}) %all-to-all-start) | async-done | bytes 393248 | tf_op jit(solution)/shard_map/all_to_all | solution.py:165
  61.7 0.2 reshape.113.x_ref
  61.9 1.3 gram_blocks.1
  63.2 7.0 %all-to-all-start.1 = ((f32[16,80,128]{2,1,0:T(8,128)}), f32[16,80,128]{2,1,0:T(8,128)S(1)}, u32[]{:S(2)}, u32[]{:S(2)}) async-start(f32[16,80,128]{2,1,0:T(8,128)} %bitcast), calls=%async_computation.1 | async-start | bytes 1310720 | tf_op jit(solution)/shard_map/all_to_all | solution.py:165
  70.2 0.1 pad_maximum_fusion.refs_0_
  70.3 3.3 %collective-permute-start.4 = (bf16[4,192,384]{2,1,0:T(8,128)(2,1)S(1)}, bf16[4,192,384]{2,1,0:T(8,128)(2,1)S(1)}, u32[]{:S(2)}, u32[]{:S(2)}) collective-permute-start(bf16[4,192,384]{2,1,0:T(8,128)(2,1)S(1)} %pad_maximum_fusion.refs_0_), channel_id=1, source_target_pairs={{0,128},{128,256},{256,384},{384,0},{1,129},{129,257},{257,385},{3... | collective-permute-start | bytes 1769480 | tf_op jit(solution)/shard_map/ppermute | solution.py:169
  73.6 3.2 %collective-permute-start.5 = (bf16[4,192,384]{2,1,0:T(8,128)(2,1)S(1)}, bf16[4,192,384]{2,1,0:T(8,128)(2,1)S(1)}, u32[]{:S(2)}, u32[]{:S(2)}) collective-permute-start(bf16[4,192,384]{2,1,0:T(8,128)(2,1)S(1)} %pad_maximum_fusion.refs_0_), channel_id=1, source_target_pairs={{0,384},{128,0},{256,128},{384,256},{1,385},{129,1},{257,129},{385... | collective-permute-start | bytes 1769480 | tf_op jit(solution)/shard_map/ppermute | solution.py:169
  76.9 5.8 %all-to-all-done.1.r_ref = f32[16,80,128]{2,1,0:T(8,128)S(1)} async-done(((f32[16,80,128]{2,1,0:T(8,128)}), f32[16,80,128]{2,1,0:T(8,128)S(1)}, u32[]{:S(2)}, u32[]{:S(2)}) %all-to-all-start.1) | async-done | bytes 655392 | tf_op jit(solution)/shard_map/all_to_all | solution.py:165
  82.6 0.9 sum_and_repeat.1
  83.5 3.6 %all-to-all-start.2 = ((f32[16,80,128]{2,1,0:T(8,128)}), f32[16,80,128]{2,1,0:T(8,128)S(1)}, u32[]{:S(2)}, u32[]{:S(2)}) async-start(f32[16,80,128]{2,1,0:T(8,128)} %sum_and_repeat.1), calls=%async_computation.2 | async-start | bytes 1310720 | tf_op jit(solution)/shard_map/all_to_all | solution.py:165
  87.1 0.1 add_xor_fusion
  87.2 0.1 xor.16.place_ref
  87.3 1.7 abs_reduce_fusion
  88.9 0.3 abs_reduce_fusion.1
  89.3 0.1 broadcast_in_dim.15
  89.3 0.1 broadcast_in_dim.16
  89.5 7.3 %collective-permute-done.4.refs_1_ = bf16[4,192,384]{2,1,0:T(8,128)(2,1)S(1)} collective-permute-done((bf16[4,192,384]{2,1,0:T(8,128)(2,1)S(1)}, bf16[4,192,384]{2,1,0:T(8,128)(2,1)S(1)}, u32[]{:S(2)}, u32[]{:S(2)}) %collective-permute-start.4) | collective-permute-done | bytes 589856 | tf_op jit(solution)/shard_map/ppermute | solution.py:169
  96.7 1.4 collective-permute-done.5.refs_3_
  98.1 2.3 %all-to-all-done.2 = f32[16,80,128]{2,1,0:T(8,128)S(1)} async-done(((f32[16,80,128]{2,1,0:T(8,128)}), f32[16,80,128]{2,1,0:T(8,128)S(1)}, u32[]{:S(2)}, u32[]{:S(2)}) %all-to-all-start.2) | async-done | bytes 655392 | tf_op jit(solution)/shard_map/all_to_all | solution.py:165
  100.4 0.1 copy.6.lift_ref
  100.6 3.0 %collective-permute-start.6 = (bf16[4,192,384]{2,1,0:T(8,128)(2,1)S(1)}, bf16[4,192,384]{2,1,0:T(8,128)(2,1)}, u32[]{:S(2)}, u32[]{:S(2)}) collective-permute-start(bf16[4,192,384]{2,1,0:T(8,128)(2,1)S(1)} %collective-permute-done.4.refs_1_), channel_id=1, source_target_pairs={{0,128},{128,256},{256,384},{384,0},{1,129},{129,257},{257,385},{3... | collective-permute-start | bytes 1769480 | tf_op jit(solution)/shard_map/ppermute | solution.py:169
  103.6 8.2 %newton.1 = f32[384,512]{1,0:T(8,128)S(1)} custom-call(f32[1280,128]{1,0:T(8,128)S(1)} %bitcast.8, bf16[384,512]{1,0:T(8,128)(2,1)S(1)} %reshape.113.x_ref, f32[384,1]{1,0:T(8,128)S(1)} %copy.6.lift_ref), custom_call_target="tpu_custom_call" | custom-call | flops 7247757312 | bytes 3145728 | tf_op jit(solution)/shard_map/newton/pallas_call | solution.py:122
  111.8 0.1 convert_element_type.16
  111.8 1.0 reshape.116
  112.8 9.9 %all-to-all-start.3 = ((f16[32,48,128]{2,1,0:T(8,128)(2,1)}), f16[32,48,128]{2,1,0:T(8,128)(2,1)}, u32[]{:S(2)}, u32[]{:S(2)}) async-start(f16[32,48,128]{2,1,0:T(8,128)(2,1)} %reshape.116), calls=%async_computation.3 | async-start | bytes 786432 | tf_op jit(solution)/shard_map/all_to_all | solution.py:165
  122.8 0.0 collective-permute-done.6.refs_2_
  122.8 0.0 all-gather.2.cloned.1.call-done
  122.8 0.0 copy-start
  122.8 1.9 %copy-done = bf16[4096,384]{1,0:T(8,128)(2,1)S(1)} copy-done((bf16[4096,384]{1,0:T(8,128)(2,1)S(1)}, bf16[4096,384]{1,0:T(8,128)(2,1)}, u32[]{:S(2)}) %copy-start) | copy-done | bytes 3145752
  124.7 0.0 copy-start.1
  124.7 3.1 %project.1 = (f32[128,192]{1,0:T(8,128)S(1)}, f32[128,192]{1,0:T(8,128)S(1)}) custom-call(s32[1]{0:T(128)} %bitcast.6.zh_ref, s32[16]{0:T(128)S(1)} %xor.16.place_ref, bf16[2,16,128,384]{3,2,1,0:T(8,128)(2,1)S(1)} %bitcast.10, bf16[4,192,384]{2,1,0:T(8,128)(2,1)S(1)} %pad_maximum_fusion.refs_0_, bf16[4,192,384]{2,1,0:T(8,128)(2,1)S(1)} %collective-permute-done.4.refs_1_, ...), custom_call_target="tpu_custom_call" | custom-call | flops 999999995904 | bytes 6291456 | tf_op jit(solution)/shard_map/project/pallas_call | solution.py:149
  127.8 12.0 %collective-permute-start.7 = (f32[128,192]{1,0:T(8,128)S(1)}, f32[128,192]{1,0:T(8,128)S(1)}, u32[]{:S(2)}, u32[]{:S(2)}) collective-permute-start(f32[128,192]{1,0:T(8,128)S(1)} %get-tuple-element.24), channel_id=1, source_target_pairs={{0,16},{16,0},{1,17},{17,1},{2,18},{18,2},{3,19},{19,3},{4,20},{20... | collective-permute-start | bytes 294920 | tf_op jit(solution)/shard_map/ppermute | solution.py:222
  139.8 0.0 copy-done.1
  139.9 11.2 %all-to-all-done.3 = f16[32,48,128]{2,1,0:T(8,128)(2,1)} async-done(((f16[32,48,128]{2,1,0:T(8,128)(2,1)}), f16[32,48,128]{2,1,0:T(8,128)(2,1)}, u32[]{:S(2)}, u32[]{:S(2)}) %all-to-all-start.3) | async-done | bytes 393248 | tf_op jit(solution)/shard_map/all_to_all | solution.py:165
  151.1 11.1 %collective-permute-done.7 = f32[128,192]{1,0:T(8,128)S(1)} collective-permute-done((f32[128,192]{1,0:T(8,128)S(1)}, f32[128,192]{1,0:T(8,128)S(1)}, u32[]{:S(2)}, u32[]{:S(2)}) %collective-permute-start.7) | collective-permute-done | bytes 98336 | tf_op jit(solution)/shard_map/ppermute | solution.py:222
  162.2 1.0 convert_element_type.20
  163.2 0.1 reshape.119
  163.4 0.1 broadcast_multiply_fusion
  163.5 1.3 copy.7
  164.9 0.8 pad_maximum_fusion.1
  (5 shorter events, 0.1 us)
Async XLA Ops:
  7.2 28.9 %collective-permute-start = (bf16[192,384]{1,0:T(8,128)(2,1)}, bf16[192,384]{1,0:T(8,128)(2,1)S(1)}, u32[]{:S(2)}, u32[]{:S(2)}) collective-permute-start(bf16[192,384]{1,0:T(8,128)(2,1)} %param.5), channel_id=1, source_target_pairs={{0,0},{1,32},{2,64},{3,96},{4,128},{5,160},{6,192},{7,224},{8,256}... | collective-permute-start | bytes 442376 | tf_op jit(solution)/shard_map/ppermute | solution.py:186
  13.9 47.8 %all-to-all-start = ((bf16[32,48,128]{2,1,0:T(8,128)(2,1)}), bf16[32,48,128]{2,1,0:T(8,128)(2,1)S(1)}, u32[]{:S(2)}, u32[]{:S(2)}) async-start(bf16[32,48,128]{2,1,0:T(8,128)(2,1)} %reshape.112), calls=%async_computation | async-start | bytes 786432 | tf_op jit(solution)/shard_map/all_to_all | solution.py:165
  33.7 89.1 %all-gather.2.cloned.1.call-start = ((), (), s32[]{:S(2)}) async-start(), calls=%async_computation.4 | async-start | bytes 3244032 | tf_op jit(solution)/shard_map/all_gather | solution.py:200
  36.0 8.4 %collective-permute-start.1 = (bf16[192,384]{1,0:T(8,128)(2,1)S(1)}, bf16[192,384]{1,0:T(8,128)(2,1)S(1)}, u32[]{:S(2)}, u32[]{:S(2)}) collective-permute-start(bf16[192,384]{1,0:T(8,128)(2,1)S(1)} %relay.1), channel_id=1, source_target_pairs={{0,32},{32,64},{64,96},{96,0},{1,33},{33,65},{65,97},{97,1},{2,34}... | collective-permute-start | bytes 442376 | tf_op jit(solution)/shard_map/ppermute | solution.py:169
  38.0 7.7 %collective-permute-start.2 = (bf16[192,384]{1,0:T(8,128)(2,1)S(1)}, bf16[192,384]{1,0:T(8,128)(2,1)S(1)}, u32[]{:S(2)}, u32[]{:S(2)}) collective-permute-start(bf16[192,384]{1,0:T(8,128)(2,1)S(1)} %relay.1), channel_id=1, source_target_pairs={{0,64},{32,96},{64,0},{96,32},{1,65},{33,97},{65,1},{97,33},{2,66}... | collective-permute-start | bytes 442376 | tf_op jit(solution)/shard_map/ppermute | solution.py:169
  39.9 8.0 %collective-permute-start.3 = (bf16[192,384]{1,0:T(8,128)(2,1)S(1)}, bf16[192,384]{1,0:T(8,128)(2,1)S(1)}, u32[]{:S(2)}, u32[]{:S(2)}) collective-permute-start(bf16[192,384]{1,0:T(8,128)(2,1)S(1)} %relay.1), channel_id=1, source_target_pairs={{0,96},{32,0},{64,32},{96,64},{1,97},{33,1},{65,33},{97,65},{2,98}... | collective-permute-start | bytes 442376 | tf_op jit(solution)/shard_map/ppermute | solution.py:169
  63.2 19.4 %all-to-all-start.1 = ((f32[16,80,128]{2,1,0:T(8,128)}), f32[16,80,128]{2,1,0:T(8,128)S(1)}, u32[]{:S(2)}, u32[]{:S(2)}) async-start(f32[16,80,128]{2,1,0:T(8,128)} %bitcast), calls=%async_computation.1 | async-start | bytes 1310720 | tf_op jit(solution)/shard_map/all_to_all | solution.py:165
  70.3 26.4 %collective-permute-start.4 = (bf16[4,192,384]{2,1,0:T(8,128)(2,1)S(1)}, bf16[4,192,384]{2,1,0:T(8,128)(2,1)S(1)}, u32[]{:S(2)}, u32[]{:S(2)}) collective-permute-start(bf16[4,192,384]{2,1,0:T(8,128)(2,1)S(1)} %pad_maximum_fusion.refs_0_), channel_id=1, source_target_pairs={{0,128},{128,256},{256,384},{384,0},{1,129},{129,257},{257,385},{3... | collective-permute-start | bytes 1769480 | tf_op jit(solution)/shard_map/ppermute | solution.py:169
  73.6 24.5 %collective-permute-start.5 = (bf16[4,192,384]{2,1,0:T(8,128)(2,1)S(1)}, bf16[4,192,384]{2,1,0:T(8,128)(2,1)S(1)}, u32[]{:S(2)}, u32[]{:S(2)}) collective-permute-start(bf16[4,192,384]{2,1,0:T(8,128)(2,1)S(1)} %pad_maximum_fusion.refs_0_), channel_id=1, source_target_pairs={{0,384},{128,0},{256,128},{384,256},{1,385},{129,1},{257,129},{385... | collective-permute-start | bytes 1769480 | tf_op jit(solution)/shard_map/ppermute | solution.py:169
  83.5 16.9 %all-to-all-start.2 = ((f32[16,80,128]{2,1,0:T(8,128)}), f32[16,80,128]{2,1,0:T(8,128)S(1)}, u32[]{:S(2)}, u32[]{:S(2)}) async-start(f32[16,80,128]{2,1,0:T(8,128)} %sum_and_repeat.1), calls=%async_computation.2 | async-start | bytes 1310720 | tf_op jit(solution)/shard_map/all_to_all | solution.py:165
  100.6 22.2 %collective-permute-start.6 = (bf16[4,192,384]{2,1,0:T(8,128)(2,1)S(1)}, bf16[4,192,384]{2,1,0:T(8,128)(2,1)}, u32[]{:S(2)}, u32[]{:S(2)}) collective-permute-start(bf16[4,192,384]{2,1,0:T(8,128)(2,1)S(1)} %collective-permute-done.4.refs_1_), channel_id=1, source_target_pairs={{0,128},{128,256},{256,384},{384,0},{1,129},{129,257},{257,385},{3... | collective-permute-start | bytes 1769480 | tf_op jit(solution)/shard_map/ppermute | solution.py:169
  112.8 38.3 %all-to-all-start.3 = ((f16[32,48,128]{2,1,0:T(8,128)(2,1)}), f16[32,48,128]{2,1,0:T(8,128)(2,1)}, u32[]{:S(2)}, u32[]{:S(2)}) async-start(f16[32,48,128]{2,1,0:T(8,128)(2,1)} %reshape.116), calls=%async_computation.3 | async-start | bytes 786432 | tf_op jit(solution)/shard_map/all_to_all | solution.py:165
  122.8 1.9 %copy-start = (bf16[4096,384]{1,0:T(8,128)(2,1)S(1)}, bf16[4096,384]{1,0:T(8,128)(2,1)}, u32[]{:S(2)}) copy-start(bf16[4096,384]{1,0:T(8,128)(2,1)} %all-gather.2.cloned.1.call-done) | copy-start | bytes 9437188
  124.7 15.1 %copy-start.1 = (f32[32]{0:T(128)S(1)}, f32[32]{0:T(128)}, u32[]{:S(2)}) copy-start(f32[32]{0:T(128)} %abs_reduce_fusion) | copy-start | bytes 388
  127.8 34.4 %collective-permute-start.7 = (f32[128,192]{1,0:T(8,128)S(1)}, f32[128,192]{1,0:T(8,128)S(1)}, u32[]{:S(2)}, u32[]{:S(2)}) collective-permute-start(f32[128,192]{1,0:T(8,128)S(1)} %get-tuple-element.24), channel_id=1, source_target_pairs={{0,16},{16,0},{1,17},{17,1},{2,18},{18,2},{3,19},{19,3},{4,20},{20... | collective-permute-start | bytes 294920 | tf_op jit(solution)/shard_map/ppermute | solution.py:222
Sparse Core Ops, SparseCore 0:
  36.7 74.1 all-gather.1

commit v3 on v2

--- a/solution.py
+++ b/solution.py
@@ -156,6 +156,25 @@
     )(zh, place, q, *ws)
 
 
+def unpack_kernel(scale_ref, x_ref, o_ref):
+    mats, rows, columns = o_ref.shape
+    for m in range(mats):
+        x = x_ref[m] * scale_ref[m]
+        for c in range(columns // BLK):
+            o_ref[m, :, c * BLK : (c + 1) * BLK] = x[c * rows : (c + 1) * rows]
+
+
+def unpack(scale, x, shape):
+    return pl.pallas_call(
+        unpack_kernel,
+        in_specs=[pl.BlockSpec(memory_space=pltpu.SMEM), pl.BlockSpec(memory_space=pltpu.VMEM)],
+        out_shape=jax.ShapeDtypeStruct(shape, F32),
+        compiler_params=params(16),
+        cost_estimate=pl.CostEstimate(flops=1, bytes_accessed=1, transcendentals=0),
+        name="unpack",
+    )(scale, x)
+
+
 def chunk_scale(rows):
     top = jnp.max(jnp.abs(rows.astype(F32)), axis=(1, 2), keepdims=True)
     return jnp.where((top < TINY) & (top > 0.0), TINY / jnp.maximum(top, 2.0**-126), 1.0)
@@ -208,7 +227,7 @@
     result = newton(gram, rows, lift)
     (opposite,) = round_ring(behind, "y", (1,))
     weights = [along_x, behind, opposite, ahead]
-    sent = result.astype(jnp.float16).reshape(packed)
+    sent = result.astype(jnp.float16).reshape(mats, own_rows, kv // BLK, BLK).transpose(0, 2, 1, 3).reshape(packed)
     returned = exchange(sent, COLUMN)
 
     tokens, heads = d_query.shape
@@ -219,8 +238,9 @@
         queries.reshape(sizes["zh"], line, tokens, heads),
         weights,
     )
-    returned, swapped = lax.optimization_barrier((returned, lax.ppermute(other, "zh", [(0, 1), (1, 0)])))
-    updates = returned.reshape(grads.shape).astype(F32) * (1.0 / (HALF_SCALE * chunk_scale(grads)))
+    swapped = lax.ppermute(other, "zh", [(0, 1), (1, 0)])
+    returned, own = lax.optimization_barrier((returned, own))
+    updates = unpack((1.0 / (HALF_SCALE * chunk_scale(grads))).reshape(mats), returned.astype(F32), grads.shape)
     first = zh == 0
     d_input = jnp.concatenate([jnp.where(first, own, swapped), jnp.where(first, swapped, own)], axis=1)
     return updates, d_input

time: 173 us -> 171 us (0.988)
  waiting for transfers between devices: 58.5 us -> 55.5 us
    ppermute x1, waiting for transfers between devices: 11.1 us -> 8.07 us  [body(): swapped = lax.ppermute(other, 'zh', [(0, 1), (1, 0)])]
  transfers between devices with their start and end apart: 13 -> 13, of which waited for: 10 -> 10; matrix products, arithmetic and copies ran while one was open for 4% -> 5% of each run, Pallas kernels for 8% -> 8%
where the time goes in v3:
time: 171 us; the launch traced here: 170 us
  starting transfers between devices  74.8 us (44%)
  waiting for transfers between devices  55.5 us (32%)
  between operations  14.3 us (8%)
  Pallas kernels  14.1 us (8%)
  local copies, waits for them, and re-layouts  7.25 us (4%)
  other arithmetic  4.09 us (2%)
    all_to_all x4, starting transfers between devices, exchange(): return lax.all_to_all(x, axes, split_axis=0, concat_axis=0, tiled=True)  40.3 us
    all_to_all x4, waiting for transfers between devices, exchange(): return lax.all_to_all(x, axes, split_axis=0, concat_axis=0, tiled=True)  33.2 us
    ppermute x6, starting transfers between devices, round_ring(): lax.ppermute(x, axis, [(i, (i + k) % 4) for i in range(4)])  17.9 us
    ppermute x6, waiting for transfers between devices, round_ring(): lax.ppermute(x, axis, [(i, (i + k) % 4) for i in range(4)])  12 us
    ppermute x1, starting transfers between devices, body(): swapped = lax.ppermute(other, 'zh', [(0, 1), (1, 0)])  12 us
    pallas_call x1, Pallas kernels, newton(): pl.pallas_call(newton_kernel, out_shape=jax.ShapeDtypeStruct(x.shape, F32...  8.16 us
    ppermute x1, waiting for transfers between devices, body(): swapped = lax.ppermute(other, 'zh', [(0, 1), (1, 0)])  8.07 us
    ppermute x1, starting transfers between devices, body(): turned = lax.ppermute(w_query, ('y', 'x', 'zl', 'core'), turn(sizes))  4.51 us
  transfers between devices with their start and end apart: 13, of which 10 were waited for; matrix products, arithmetic and copies ran while one was open for 5% of the time, Pallas kernels for 8%

profile of v3, /device:TPU:1, one launch (start us, length us, event | category | flops | bytes accessed | tf_op | source)
XLA Modules:
  0.0 170.0 jit_solution(2883915943029121290)
XLA Ops:
  7.2 4.5 %collective-permute-start = (bf16[192,384]{1,0:T(8,128)(2,1)}, bf16[192,384]{1,0:T(8,128)(2,1)S(1)}, u32[]{:S(2)}, u32[]{:S(2)}) collective-permute-start(bf16[192,384]{1,0:T(8,128)(2,1)} %param.5), channel_id=1, source_target_pairs={{0,0},{1,32},{2,64},{3,96},{4,128},{5,160},{6,192},{7,224},{8,256}... | collective-permute-start | bytes 442376 | tf_op jit(solution)/shard_map/ppermute | solution.py:205
  11.7 1.2 copy.7
  12.9 1.0 reshape.104
  13.9 19.8 %all-to-all-start = ((bf16[32,48,128]{2,1,0:T(8,128)(2,1)}), bf16[32,48,128]{2,1,0:T(8,128)(2,1)S(1)}, u32[]{:S(2)}, u32[]{:S(2)}) async-start(bf16[32,48,128]{2,1,0:T(8,128)(2,1)} %reshape.104), calls=%async_computation | async-start | bytes 786432 | tf_op jit(solution)/shard_map/all_to_all | solution.py:184
  33.7 0.0 all-gather.2.cloned.1.call-start
  33.8 0.7 all-gather.2.cloned.1.call-update
  34.4 1.6 collective-permute-done.x_ref
  36.0 1.9 %collective-permute-start.1 = (bf16[192,384]{1,0:T(8,128)(2,1)S(1)}, bf16[192,384]{1,0:T(8,128)(2,1)S(1)}, u32[]{:S(2)}, u32[]{:S(2)}) collective-permute-start(bf16[192,384]{1,0:T(8,128)(2,1)S(1)} %relay.1), channel_id=1, source_target_pairs={{0,32},{32,64},{64,96},{96,0},{1,33},{33,65},{65,97},{97,1},{2,34}... | collective-permute-start | bytes 442376 | tf_op jit(solution)/shard_map/ppermute | solution.py:188
  38.0 1.9 %collective-permute-start.2 = (bf16[192,384]{1,0:T(8,128)(2,1)S(1)}, bf16[192,384]{1,0:T(8,128)(2,1)S(1)}, u32[]{:S(2)}, u32[]{:S(2)}) collective-permute-start(bf16[192,384]{1,0:T(8,128)(2,1)S(1)} %relay.1), channel_id=1, source_target_pairs={{0,64},{32,96},{64,0},{96,32},{1,65},{33,97},{65,1},{97,33},{2,66}... | collective-permute-start | bytes 442376 | tf_op jit(solution)/shard_map/ppermute | solution.py:188
  39.9 4.6 %collective-permute-start.3 = (bf16[192,384]{1,0:T(8,128)(2,1)S(1)}, bf16[192,384]{1,0:T(8,128)(2,1)S(1)}, u32[]{:S(2)}, u32[]{:S(2)}) collective-permute-start(bf16[192,384]{1,0:T(8,128)(2,1)S(1)} %relay.1), channel_id=1, source_target_pairs={{0,96},{32,0},{64,32},{96,64},{1,97},{33,1},{65,33},{97,65},{2,98}... | collective-permute-start | bytes 442376 | tf_op jit(solution)/shard_map/ppermute | solution.py:188
  44.5 0.0 collective-permute-done.1
  44.5 1.2 collective-permute-done.2
  45.7 2.2 %collective-permute-done.3 = bf16[192,384]{1,0:T(8,128)(2,1)S(1)} collective-permute-done((bf16[192,384]{1,0:T(8,128)(2,1)S(1)}, bf16[192,384]{1,0:T(8,128)(2,1)S(1)}, u32[]{:S(2)}, u32[]{:S(2)}) %collective-permute-start.3) | collective-permute-done | bytes 147488 | tf_op jit(solution)/shard_map/ppermute | solution.py:188
  47.9 13.8 %all-to-all-done = bf16[32,48,128]{2,1,0:T(8,128)(2,1)S(1)} async-done(((bf16[32,48,128]{2,1,0:T(8,128)(2,1)}), bf16[32,48,128]{2,1,0:T(8,128)(2,1)S(1)}, u32[]{:S(2)}, u32[]{:S(2)}) %all-to-all-start) | async-done | bytes 393248 | tf_op jit(solution)/shard_map/all_to_all | solution.py:184
  61.7 0.2 reshape.105.x_ref
  61.9 1.3 gram_blocks.1
  63.2 7.0 %all-to-all-start.1 = ((f32[16,80,128]{2,1,0:T(8,128)}), f32[16,80,128]{2,1,0:T(8,128)S(1)}, u32[]{:S(2)}, u32[]{:S(2)}) async-start(f32[16,80,128]{2,1,0:T(8,128)} %bitcast), calls=%async_computation.1 | async-start | bytes 1310720 | tf_op jit(solution)/shard_map/all_to_all | solution.py:184
  70.2 0.1 pad_maximum_fusion.refs_0_
  70.3 3.3 %collective-permute-start.4 = (bf16[4,192,384]{2,1,0:T(8,128)(2,1)S(1)}, bf16[4,192,384]{2,1,0:T(8,128)(2,1)S(1)}, u32[]{:S(2)}, u32[]{:S(2)}) collective-permute-start(bf16[4,192,384]{2,1,0:T(8,128)(2,1)S(1)} %pad_maximum_fusion.refs_0_), channel_id=1, source_target_pairs={{0,128},{128,256},{256,384},{384,0},{1,129},{129,257},{257,385},{3... | collective-permute-start | bytes 1769480 | tf_op jit(solution)/shard_map/ppermute | solution.py:188
  73.6 3.2 %collective-permute-start.5 = (bf16[4,192,384]{2,1,0:T(8,128)(2,1)S(1)}, bf16[4,192,384]{2,1,0:T(8,128)(2,1)S(1)}, u32[]{:S(2)}, u32[]{:S(2)}) collective-permute-start(bf16[4,192,384]{2,1,0:T(8,128)(2,1)S(1)} %pad_maximum_fusion.refs_0_), channel_id=1, source_target_pairs={{0,384},{128,0},{256,128},{384,256},{1,385},{129,1},{257,129},{385... | collective-permute-start | bytes 1769480 | tf_op jit(solution)/shard_map/ppermute | solution.py:188
  76.9 5.8 %all-to-all-done.1.r_ref = f32[16,80,128]{2,1,0:T(8,128)S(1)} async-done(((f32[16,80,128]{2,1,0:T(8,128)}), f32[16,80,128]{2,1,0:T(8,128)S(1)}, u32[]{:S(2)}, u32[]{:S(2)}) %all-to-all-start.1) | async-done | bytes 655392 | tf_op jit(solution)/shard_map/all_to_all | solution.py:184
  82.6 0.9 sum_and_repeat.1
  83.5 3.6 %all-to-all-start.2 = ((f32[16,80,128]{2,1,0:T(8,128)}), f32[16,80,128]{2,1,0:T(8,128)S(1)}, u32[]{:S(2)}, u32[]{:S(2)}) async-start(f32[16,80,128]{2,1,0:T(8,128)} %sum_and_repeat.1), calls=%async_computation.2 | async-start | bytes 1310720 | tf_op jit(solution)/shard_map/all_to_all | solution.py:184
  87.1 0.1 add_xor_fusion
  87.2 0.1 xor.16.place_ref
  87.3 1.7 abs_reduce_fusion.1
  88.9 0.3 abs_reduce_fusion
  89.3 0.1 broadcast_in_dim.12
  89.3 0.1 broadcast_in_dim.13
  89.5 7.3 %collective-permute-done.4.refs_1_ = bf16[4,192,384]{2,1,0:T(8,128)(2,1)S(1)} collective-permute-done((bf16[4,192,384]{2,1,0:T(8,128)(2,1)S(1)}, bf16[4,192,384]{2,1,0:T(8,128)(2,1)S(1)}, u32[]{:S(2)}, u32[]{:S(2)}) %collective-permute-start.4) | collective-permute-done | bytes 589856 | tf_op jit(solution)/shard_map/ppermute | solution.py:188
  96.7 1.4 collective-permute-done.5.refs_3_
  98.1 2.3 %all-to-all-done.2 = f32[16,80,128]{2,1,0:T(8,128)S(1)} async-done(((f32[16,80,128]{2,1,0:T(8,128)}), f32[16,80,128]{2,1,0:T(8,128)S(1)}, u32[]{:S(2)}, u32[]{:S(2)}) %all-to-all-start.2) | async-done | bytes 655392 | tf_op jit(solution)/shard_map/all_to_all | solution.py:184
  100.4 0.1 copy.8.lift_ref
  100.6 3.0 %collective-permute-start.6 = (bf16[4,192,384]{2,1,0:T(8,128)(2,1)S(1)}, bf16[4,192,384]{2,1,0:T(8,128)(2,1)}, u32[]{:S(2)}, u32[]{:S(2)}) collective-permute-start(bf16[4,192,384]{2,1,0:T(8,128)(2,1)S(1)} %collective-permute-done.4.refs_1_), channel_id=1, source_target_pairs={{0,128},{128,256},{256,384},{384,0},{1,129},{129,257},{257,385},{3... | collective-permute-start | bytes 1769480 | tf_op jit(solution)/shard_map/ppermute | solution.py:188
  103.6 8.2 %newton.1 = f32[384,512]{1,0:T(8,128)S(1)} custom-call(f32[1280,128]{1,0:T(8,128)S(1)} %bitcast.11, bf16[384,512]{1,0:T(8,128)(2,1)S(1)} %reshape.105.x_ref, f32[384,1]{1,0:T(8,128)S(1)} %copy.8.lift_ref), custom_call_target="tpu_custom_call" | custom-call | flops 7247757312 | bytes 3145728 | tf_op jit(solution)/shard_map/newton/pallas_call | solution.py:122
  111.8 0.1 convert_element_type.14
  111.8 0.1 reshape.108
  112.0 0.1 copy.9
  112.1 0.9 copy.10
  113.0 9.9 %all-to-all-start.3 = ((f16[32,48,128]{2,1,0:T(8,128)(2,1)}), f16[32,48,128]{2,1,0:T(8,128)(2,1)}, u32[]{:S(2)}, u32[]{:S(2)}) async-start(f16[32,48,128]{2,1,0:T(8,128)(2,1)} %copy.10), calls=%async_computation.3 | async-start | bytes 786432 | tf_op jit(solution)/shard_map/all_to_all | solution.py:184
  122.9 0.0 collective-permute-done.6.refs_2_
  122.9 0.0 all-gather.2.cloned.1.call-done
  123.0 0.0 copy-start
  123.0 1.9 %copy-done = bf16[4096,384]{1,0:T(8,128)(2,1)S(1)} copy-done((bf16[4096,384]{1,0:T(8,128)(2,1)S(1)}, bf16[4096,384]{1,0:T(8,128)(2,1)}, u32[]{:S(2)}) %copy-start) | copy-done | bytes 3145752
  124.9 0.0 copy-start.1
  124.9 3.1 %project.1 = (f32[128,192]{1,0:T(8,128)S(1)}, f32[128,192]{1,0:T(8,128)S(1)}) custom-call(s32[1]{0:T(128)} %bitcast.8.zh_ref, s32[16]{0:T(128)S(1)} %xor.16.place_ref, bf16[2,16,128,384]{3,2,1,0:T(8,128)(2,1)S(1)} %bitcast.13, bf16[4,192,384]{2,1,0:T(8,128)(2,1)S(1)} %pad_maximum_fusion.refs_0_, bf16[4,192,384]{2,1,0:T(8,128)(2,1)S(1)} %collective-permute-done.4.refs_1_, ...), custom_call_target="tpu_custom_call" | custom-call | flops 999999995904 | bytes 6291456 | tf_op jit(solution)/shard_map/project/pallas_call | solution.py:149
  128.0 12.0 %collective-permute-start.7 = (f32[128,192]{1,0:T(8,128)S(1)}, f32[128,192]{1,0:T(8,128)S(1)}, u32[]{:S(2)}, u32[]{:S(2)}) collective-permute-start(f32[128,192]{1,0:T(8,128)S(1)} %get-tuple-element.27), channel_id=1, source_target_pairs={{0,16},{16,0},{1,17},{17,1},{2,18},{18,2},{3,19},{19,3},{4,20},{20... | collective-permute-start | bytes 294920 | tf_op jit(solution)/shard_map/ppermute | solution.py:241
  140.0 0.0 copy-done.1
  140.0 11.2 %all-to-all-done.3 = f16[32,48,128]{2,1,0:T(8,128)(2,1)} async-done(((f16[32,48,128]{2,1,0:T(8,128)(2,1)}), f16[32,48,128]{2,1,0:T(8,128)(2,1)}, u32[]{:S(2)}, u32[]{:S(2)}) %all-to-all-start.3) | async-done | bytes 393248 | tf_op jit(solution)/shard_map/all_to_all | solution.py:184
  151.3 1.0 convert_element_type.15.x_ref
  152.3 0.6 unpack.1
  153.0 1.3 copy.11
  154.3 8.1 %collective-permute-done.7 = f32[128,192]{1,0:T(8,128)S(1)} collective-permute-done((f32[128,192]{1,0:T(8,128)S(1)}, f32[128,192]{1,0:T(8,128)S(1)}, u32[]{:S(2)}, u32[]{:S(2)}) %collective-permute-start.7) | collective-permute-done | bytes 98336 | tf_op jit(solution)/shard_map/ppermute | solution.py:241
  162.4 0.8 pad_maximum_fusion.1
  (5 shorter events, 0.1 us)
Async XLA Ops:
  7.2 28.9 %collective-permute-start = (bf16[192,384]{1,0:T(8,128)(2,1)}, bf16[192,384]{1,0:T(8,128)(2,1)S(1)}, u32[]{:S(2)}, u32[]{:S(2)}) collective-permute-start(bf16[192,384]{1,0:T(8,128)(2,1)} %param.5), channel_id=1, source_target_pairs={{0,0},{1,32},{2,64},{3,96},{4,128},{5,160},{6,192},{7,224},{8,256}... | collective-permute-start | bytes 442376 | tf_op jit(solution)/shard_map/ppermute | solution.py:205
  13.9 47.8 %all-to-all-start = ((bf16[32,48,128]{2,1,0:T(8,128)(2,1)}), bf16[32,48,128]{2,1,0:T(8,128)(2,1)S(1)}, u32[]{:S(2)}, u32[]{:S(2)}) async-start(bf16[32,48,128]{2,1,0:T(8,128)(2,1)} %reshape.104), calls=%async_computation | async-start | bytes 786432 | tf_op jit(solution)/shard_map/all_to_all | solution.py:184
  33.7 89.3 %all-gather.2.cloned.1.call-start = ((), (), s32[]{:S(2)}) async-start(), calls=%async_computation.4 | async-start | bytes 3244032 | tf_op jit(solution)/shard_map/all_gather | solution.py:219
  36.0 8.4 %collective-permute-start.1 = (bf16[192,384]{1,0:T(8,128)(2,1)S(1)}, bf16[192,384]{1,0:T(8,128)(2,1)S(1)}, u32[]{:S(2)}, u32[]{:S(2)}) collective-permute-start(bf16[192,384]{1,0:T(8,128)(2,1)S(1)} %relay.1), channel_id=1, source_target_pairs={{0,32},{32,64},{64,96},{96,0},{1,33},{33,65},{65,97},{97,1},{2,34}... | collective-permute-start | bytes 442376 | tf_op jit(solution)/shard_map/ppermute | solution.py:188
  38.0 7.7 %collective-permute-start.2 = (bf16[192,384]{1,0:T(8,128)(2,1)S(1)}, bf16[192,384]{1,0:T(8,128)(2,1)S(1)}, u32[]{:S(2)}, u32[]{:S(2)}) collective-permute-start(bf16[192,384]{1,0:T(8,128)(2,1)S(1)} %relay.1), channel_id=1, source_target_pairs={{0,64},{32,96},{64,0},{96,32},{1,65},{33,97},{65,1},{97,33},{2,66}... | collective-permute-start | bytes 442376 | tf_op jit(solution)/shard_map/ppermute | solution.py:188
  39.9 8.0 %collective-permute-start.3 = (bf16[192,384]{1,0:T(8,128)(2,1)S(1)}, bf16[192,384]{1,0:T(8,128)(2,1)S(1)}, u32[]{:S(2)}, u32[]{:S(2)}) collective-permute-start(bf16[192,384]{1,0:T(8,128)(2,1)S(1)} %relay.1), channel_id=1, source_target_pairs={{0,96},{32,0},{64,32},{96,64},{1,97},{33,1},{65,33},{97,65},{2,98}... | collective-permute-start | bytes 442376 | tf_op jit(solution)/shard_map/ppermute | solution.py:188
  63.2 19.4 %all-to-all-start.1 = ((f32[16,80,128]{2,1,0:T(8,128)}), f32[16,80,128]{2,1,0:T(8,128)S(1)}, u32[]{:S(2)}, u32[]{:S(2)}) async-start(f32[16,80,128]{2,1,0:T(8,128)} %bitcast), calls=%async_computation.1 | async-start | bytes 1310720 | tf_op jit(solution)/shard_map/all_to_all | solution.py:184
  70.3 26.4 %collective-permute-start.4 = (bf16[4,192,384]{2,1,0:T(8,128)(2,1)S(1)}, bf16[4,192,384]{2,1,0:T(8,128)(2,1)S(1)}, u32[]{:S(2)}, u32[]{:S(2)}) collective-permute-start(bf16[4,192,384]{2,1,0:T(8,128)(2,1)S(1)} %pad_maximum_fusion.refs_0_), channel_id=1, source_target_pairs={{0,128},{128,256},{256,384},{384,0},{1,129},{129,257},{257,385},{3... | collective-permute-start | bytes 1769480 | tf_op jit(solution)/shard_map/ppermute | solution.py:188
  73.6 24.5 %collective-permute-start.5 = (bf16[4,192,384]{2,1,0:T(8,128)(2,1)S(1)}, bf16[4,192,384]{2,1,0:T(8,128)(2,1)S(1)}, u32[]{:S(2)}, u32[]{:S(2)}) collective-permute-start(bf16[4,192,384]{2,1,0:T(8,128)(2,1)S(1)} %pad_maximum_fusion.refs_0_), channel_id=1, source_target_pairs={{0,384},{128,0},{256,128},{384,256},{1,385},{129,1},{257,129},{385... | collective-permute-start | bytes 1769480 | tf_op jit(solution)/shard_map/ppermute | solution.py:188
  83.5 16.9 %all-to-all-start.2 = ((f32[16,80,128]{2,1,0:T(8,128)}), f32[16,80,128]{2,1,0:T(8,128)S(1)}, u32[]{:S(2)}, u32[]{:S(2)}) async-start(f32[16,80,128]{2,1,0:T(8,128)} %sum_and_repeat.1), calls=%async_computation.2 | async-start | bytes 1310720 | tf_op jit(solution)/shard_map/all_to_all | solution.py:184
  100.6 22.4 %collective-permute-start.6 = (bf16[4,192,384]{2,1,0:T(8,128)(2,1)S(1)}, bf16[4,192,384]{2,1,0:T(8,128)(2,1)}, u32[]{:S(2)}, u32[]{:S(2)}) collective-permute-start(bf16[4,192,384]{2,1,0:T(8,128)(2,1)S(1)} %collective-permute-done.4.refs_1_), channel_id=1, source_target_pairs={{0,128},{128,256},{256,384},{384,0},{1,129},{129,257},{257,385},{3... | collective-permute-start | bytes 1769480 | tf_op jit(solution)/shard_map/ppermute | solution.py:188
  113.0 38.3 %all-to-all-start.3 = ((f16[32,48,128]{2,1,0:T(8,128)(2,1)}), f16[32,48,128]{2,1,0:T(8,128)(2,1)}, u32[]{:S(2)}, u32[]{:S(2)}) async-start(f16[32,48,128]{2,1,0:T(8,128)(2,1)} %copy.10), calls=%async_computation.3 | async-start | bytes 786432 | tf_op jit(solution)/shard_map/all_to_all | solution.py:184
  123.0 1.9 %copy-start = (bf16[4096,384]{1,0:T(8,128)(2,1)S(1)}, bf16[4096,384]{1,0:T(8,128)(2,1)}, u32[]{:S(2)}) copy-start(bf16[4096,384]{1,0:T(8,128)(2,1)} %all-gather.2.cloned.1.call-done) | copy-start | bytes 9437188
  124.9 15.1 %copy-start.1 = (f32[32]{0:T(128)S(1)}, f32[32]{0:T(128)}, u32[]{:S(2)}) copy-start(f32[32]{0:T(128)} %abs_reduce_fusion.1) | copy-start | bytes 388
  128.0 34.4 %collective-permute-start.7 = (f32[128,192]{1,0:T(8,128)S(1)}, f32[128,192]{1,0:T(8,128)S(1)}, u32[]{:S(2)}, u32[]{:S(2)}) collective-permute-start(f32[128,192]{1,0:T(8,128)S(1)} %get-tuple-element.27), channel_id=1, source_target_pairs={{0,16},{16,0},{1,17},{17,1},{2,18},{18,2},{3,19},{19,3},{4,20},{20... | collective-permute-start | bytes 294920 | tf_op jit(solution)/shard_map/ppermute | solution.py:241
Sparse Core Ops, SparseCore 0:
  36.7 74.1 all-gather.1

commit v4 on v3

--- a/solution.py
+++ b/solution.py
@@ -81,6 +81,11 @@
 def two(x):
     high = x.astype(BF16)
     return high, (x - high.astype(F32)).astype(BF16)
+
+
+def half_exponent(x):
+    top = jnp.max(jnp.abs(x), keepdims=True)
+    return jnp.clip(jnp.round(13.0 - jnp.log2(jnp.maximum(top, 2.0**-120))), -20.0, 120.0)
 
 
 def mm(a, b):
@@ -133,12 +138,18 @@
     w_refs, (own_ref, other_ref) = refs[:-2], refs[-2:]
     zh = zh_ref[0]
     for ref, half in ((other_ref, 1 - zh), (own_ref, zh)):
-        total = jnp.zeros(ref.shape, F32)
+        total = jnp.zeros(own_ref.shape, F32)
         for i, w_ref in enumerate(w_refs):
             for j in range(w_ref.shape[0]):
                 q = q_ref[half, place_ref[i * w_ref.shape[0] + j]]
                 total += lax.dot_general(q, w_ref[j], (((1,), (1,)), ((), ())), preferred_element_type=F32)
-        ref[...] = total
+        if ref is own_ref:
+            ref[...] = total
+        else:
+            exponent = half_exponent(total)
+            tokens = total.shape[0]
+            ref[:tokens] = total * jnp.exp2(exponent)
+            ref[tokens:] = jnp.broadcast_to(exponent, (ref.shape[0] - tokens, ref.shape[1]))
 
 
 def project(zh, place, q, ws):
@@ -149,7 +160,7 @@
     return pl.pallas_call(
         project_kernel,
         in_specs=[scalars, scalars] + [pl.BlockSpec(memory_space=pltpu.VMEM)] * (1 + len(ws)),
-        out_shape=[out, out],
+        out_shape=[out, jax.ShapeDtypeStruct((tokens + 16, features), F32)],
         compiler_params=params(24),
         cost_estimate=pl.CostEstimate(flops=10**12, bytes_accessed=6 << 20, transcendentals=0),
         name="project",
@@ -238,7 +249,8 @@
         queries.reshape(sizes["zh"], line, tokens, heads),
         weights,
     )
-    swapped = lax.ppermute(other, "zh", [(0, 1), (1, 0)])
+    swapped = lax.ppermute(other.astype(jnp.float16), "zh", [(0, 1), (1, 0)]).astype(F32)
+    swapped = swapped[:-16] * jnp.exp2(-swapped[-1:, :1])
     returned, own = lax.optimization_barrier((returned, own))
     updates = unpack((1.0 / (HALF_SCALE * chunk_scale(grads))).reshape(mats), returned.astype(F32), grads.shape)
     first = zh == 0

time: 171 us -> 167 us (0.977)
  waiting for transfers between devices: 55.5 us -> 50.3 us
    ppermute x1, waiting for transfers between devices: 8.07 us -> 3.06 us  [body(): lax.ppermute(other.astype(jnp.float16), 'zh', [(0, 1), (1, 0)]).astype(F32)]
  transfers between devices with their start and end apart: 13 -> 13, of which waited for: 10 -> 10; matrix products, arithmetic and copies ran while one was open for 5% -> 5% of each run, Pallas kernels for 8% -> 9%
where the time goes in v4:
time: 167 us; the launch traced here: 166 us
  starting transfers between devices  74.8 us (45%)
  waiting for transfers between devices  50.3 us (30%)
  between operations  15 us (9%)
  Pallas kernels  14.2 us (9%)
  local copies, waits for them, and re-layouts  7.76 us (5%)
  other arithmetic  4.12 us (2%)
    all_to_all x4, starting transfers between devices, exchange(): return lax.all_to_all(x, axes, split_axis=0, concat_axis=0, tiled=True)  40.3 us
    all_to_all x4, waiting for transfers between devices, exchange(): return lax.all_to_all(x, axes, split_axis=0, concat_axis=0, tiled=True)  33 us
    ppermute x6, starting transfers between devices, round_ring(): lax.ppermute(x, axis, [(i, (i + k) % 4) for i in range(4)])  17.9 us
    ppermute x6, waiting for transfers between devices, round_ring(): lax.ppermute(x, axis, [(i, (i + k) % 4) for i in range(4)])  12 us
    ppermute x1, starting transfers between devices, body(): lax.ppermute(other.astype(jnp.float16), 'zh', [(0, 1), (1, 0)]).astype(F32)  12 us
    pallas_call x1, Pallas kernels, newton(): pl.pallas_call(newton_kernel, out_shape=jax.ShapeDtypeStruct(x.shape, F32...  8.16 us
    ppermute x1, starting transfers between devices, body(): turned = lax.ppermute(w_query, ('y', 'x', 'zl', 'core'), turn(sizes))  4.51 us
    unnamed x6, local copies, waits for them, and re-layouts  4.45 us
  transfers between devices with their start and end apart: 13, of which 10 were waited for; matrix products, arithmetic and copies ran while one was open for 5% of the time, Pallas kernels for 9%

profile of v4, /device:TPU:1, one launch (start us, length us, event | category | flops | bytes accessed | tf_op | source)
XLA Modules:
  0.0 166.2 jit_solution(7269526338047260001)
XLA Ops:
  7.2 4.5 %collective-permute-start = (bf16[192,384]{1,0:T(8,128)(2,1)}, bf16[192,384]{1,0:T(8,128)(2,1)S(1)}, u32[]{:S(2)}, u32[]{:S(2)}) collective-permute-start(bf16[192,384]{1,0:T(8,128)(2,1)} %param.5), channel_id=1, source_target_pairs={{0,0},{1,32},{2,64},{3,96},{4,128},{5,160},{6,192},{7,224},{8,256}... | collective-permute-start | bytes 442376 | tf_op jit(solution)/shard_map/ppermute | solution.py:216
  11.7 1.2 copy.7
  12.9 1.0 reshape.104
  13.9 19.8 %all-to-all-start = ((bf16[32,48,128]{2,1,0:T(8,128)(2,1)}), bf16[32,48,128]{2,1,0:T(8,128)(2,1)S(1)}, u32[]{:S(2)}, u32[]{:S(2)}) async-start(bf16[32,48,128]{2,1,0:T(8,128)(2,1)} %reshape.104), calls=%async_computation | async-start | bytes 786432 | tf_op jit(solution)/shard_map/all_to_all | solution.py:195
  33.7 0.0 all-gather.2.cloned.1.call-start
  33.8 0.7 all-gather.2.cloned.1.call-update
  34.4 1.6 collective-permute-done.x_ref
  36.0 1.9 %collective-permute-start.1 = (bf16[192,384]{1,0:T(8,128)(2,1)S(1)}, bf16[192,384]{1,0:T(8,128)(2,1)S(1)}, u32[]{:S(2)}, u32[]{:S(2)}) collective-permute-start(bf16[192,384]{1,0:T(8,128)(2,1)S(1)} %relay.1), channel_id=1, source_target_pairs={{0,32},{32,64},{64,96},{96,0},{1,33},{33,65},{65,97},{97,1},{2,34}... | collective-permute-start | bytes 442376 | tf_op jit(solution)/shard_map/ppermute | solution.py:199
  38.0 1.9 %collective-permute-start.2 = (bf16[192,384]{1,0:T(8,128)(2,1)S(1)}, bf16[192,384]{1,0:T(8,128)(2,1)S(1)}, u32[]{:S(2)}, u32[]{:S(2)}) collective-permute-start(bf16[192,384]{1,0:T(8,128)(2,1)S(1)} %relay.1), channel_id=1, source_target_pairs={{0,64},{32,96},{64,0},{96,32},{1,65},{33,97},{65,1},{97,33},{2,66}... | collective-permute-start | bytes 442376 | tf_op jit(solution)/shard_map/ppermute | solution.py:199
  39.9 4.6 %collective-permute-start.3 = (bf16[192,384]{1,0:T(8,128)(2,1)S(1)}, bf16[192,384]{1,0:T(8,128)(2,1)S(1)}, u32[]{:S(2)}, u32[]{:S(2)}) collective-permute-start(bf16[192,384]{1,0:T(8,128)(2,1)S(1)} %relay.1), channel_id=1, source_target_pairs={{0,96},{32,0},{64,32},{96,64},{1,97},{33,1},{65,33},{97,65},{2,98}... | collective-permute-start | bytes 442376 | tf_op jit(solution)/shard_map/ppermute | solution.py:199
  44.5 0.0 collective-permute-done.1
  44.5 1.2 collective-permute-done.2
  45.7 2.2 %collective-permute-done.3 = bf16[192,384]{1,0:T(8,128)(2,1)S(1)} collective-permute-done((bf16[192,384]{1,0:T(8,128)(2,1)S(1)}, bf16[192,384]{1,0:T(8,128)(2,1)S(1)}, u32[]{:S(2)}, u32[]{:S(2)}) %collective-permute-start.3) | collective-permute-done | bytes 147488 | tf_op jit(solution)/shard_map/ppermute | solution.py:199
  47.9 13.8 %all-to-all-done = bf16[32,48,128]{2,1,0:T(8,128)(2,1)S(1)} async-done(((bf16[32,48,128]{2,1,0:T(8,128)(2,1)}), bf16[32,48,128]{2,1,0:T(8,128)(2,1)S(1)}, u32[]{:S(2)}, u32[]{:S(2)}) %all-to-all-start) | async-done | bytes 393248 | tf_op jit(solution)/shard_map/all_to_all | solution.py:195
  61.7 0.2 reshape.105.x_ref
  61.9 1.3 gram_blocks.1
  63.2 7.0 %all-to-all-start.1 = ((f32[16,80,128]{2,1,0:T(8,128)}), f32[16,80,128]{2,1,0:T(8,128)S(1)}, u32[]{:S(2)}, u32[]{:S(2)}) async-start(f32[16,80,128]{2,1,0:T(8,128)} %bitcast), calls=%async_computation.1 | async-start | bytes 1310720 | tf_op jit(solution)/shard_map/all_to_all | solution.py:195
  70.2 0.1 pad_maximum_fusion.refs_0_
  70.3 3.3 %collective-permute-start.4 = (bf16[4,192,384]{2,1,0:T(8,128)(2,1)S(1)}, bf16[4,192,384]{2,1,0:T(8,128)(2,1)S(1)}, u32[]{:S(2)}, u32[]{:S(2)}) collective-permute-start(bf16[4,192,384]{2,1,0:T(8,128)(2,1)S(1)} %pad_maximum_fusion.refs_0_), channel_id=1, source_target_pairs={{0,128},{128,256},{256,384},{384,0},{1,129},{129,257},{257,385},{3... | collective-permute-start | bytes 1769480 | tf_op jit(solution)/shard_map/ppermute | solution.py:199
  73.6 3.2 %collective-permute-start.5 = (bf16[4,192,384]{2,1,0:T(8,128)(2,1)S(1)}, bf16[4,192,384]{2,1,0:T(8,128)(2,1)S(1)}, u32[]{:S(2)}, u32[]{:S(2)}) collective-permute-start(bf16[4,192,384]{2,1,0:T(8,128)(2,1)S(1)} %pad_maximum_fusion.refs_0_), channel_id=1, source_target_pairs={{0,384},{128,0},{256,128},{384,256},{1,385},{129,1},{257,129},{385... | collective-permute-start | bytes 1769480 | tf_op jit(solution)/shard_map/ppermute | solution.py:199
  76.9 5.8 %all-to-all-done.1.r_ref = f32[16,80,128]{2,1,0:T(8,128)S(1)} async-done(((f32[16,80,128]{2,1,0:T(8,128)}), f32[16,80,128]{2,1,0:T(8,128)S(1)}, u32[]{:S(2)}, u32[]{:S(2)}) %all-to-all-start.1) | async-done | bytes 655392 | tf_op jit(solution)/shard_map/all_to_all | solution.py:195
  82.6 0.9 sum_and_repeat.1
  83.5 3.6 %all-to-all-start.2 = ((f32[16,80,128]{2,1,0:T(8,128)}), f32[16,80,128]{2,1,0:T(8,128)S(1)}, u32[]{:S(2)}, u32[]{:S(2)}) async-start(f32[16,80,128]{2,1,0:T(8,128)} %sum_and_repeat.1), calls=%async_computation.2 | async-start | bytes 1310720 | tf_op jit(solution)/shard_map/all_to_all | solution.py:195
  87.1 0.1 add_xor_fusion
  87.2 0.1 xor.16.place_ref
  87.3 1.7 %abs_reduce_fusion.1 = f32[32]{0:T(128)} fusion(bf16[32,12,512]{2,0,1:T(8,128)(2,1)} %param.3), kind=kLoop, calls=%fused_computation.1 | loop fusion | flops 589792 | bytes 393344 | tf_op jit(solution)/shard_map/reduce_max | solution.py:190
  88.9 0.3 abs_reduce_fusion
  89.3 0.1 broadcast_in_dim.12
  89.3 0.1 broadcast_in_dim.13
  89.5 7.3 %collective-permute-done.4.refs_1_ = bf16[4,192,384]{2,1,0:T(8,128)(2,1)S(1)} collective-permute-done((bf16[4,192,384]{2,1,0:T(8,128)(2,1)S(1)}, bf16[4,192,384]{2,1,0:T(8,128)(2,1)S(1)}, u32[]{:S(2)}, u32[]{:S(2)}) %collective-permute-start.4) | collective-permute-done | bytes 589856 | tf_op jit(solution)/shard_map/ppermute | solution.py:199
  96.7 1.4 collective-permute-done.5.refs_3_
  98.1 2.3 %all-to-all-done.2 = f32[16,80,128]{2,1,0:T(8,128)S(1)} async-done(((f32[16,80,128]{2,1,0:T(8,128)}), f32[16,80,128]{2,1,0:T(8,128)S(1)}, u32[]{:S(2)}, u32[]{:S(2)}) %all-to-all-start.2) | async-done | bytes 655392 | tf_op jit(solution)/shard_map/all_to_all | solution.py:195
  100.4 0.1 copy.8.lift_ref
  100.6 3.0 %collective-permute-start.6 = (bf16[4,192,384]{2,1,0:T(8,128)(2,1)S(1)}, bf16[4,192,384]{2,1,0:T(8,128)(2,1)}, u32[]{:S(2)}, u32[]{:S(2)}) collective-permute-start(bf16[4,192,384]{2,1,0:T(8,128)(2,1)S(1)} %collective-permute-done.4.refs_1_), channel_id=1, source_target_pairs={{0,128},{128,256},{256,384},{384,0},{1,129},{129,257},{257,385},{3... | collective-permute-start | bytes 1769480 | tf_op jit(solution)/shard_map/ppermute | solution.py:199
  103.6 8.2 %newton.1 = f32[384,512]{1,0:T(8,128)S(1)} custom-call(f32[1280,128]{1,0:T(8,128)S(1)} %bitcast.12, bf16[384,512]{1,0:T(8,128)(2,1)S(1)} %reshape.105.x_ref, f32[384,1]{1,0:T(8,128)S(1)} %copy.8.lift_ref), custom_call_target="tpu_custom_call" | custom-call | flops 7247757312 | bytes 3145728 | tf_op jit(solution)/shard_map/newton/pallas_call | solution.py:127
  111.8 0.1 convert_element_type.20
  111.8 0.1 reshape.108
  112.0 0.1 copy.9
  112.1 0.9 copy.10
  113.0 9.9 %all-to-all-start.3 = ((f16[32,48,128]{2,1,0:T(8,128)(2,1)}), f16[32,48,128]{2,1,0:T(8,128)(2,1)}, u32[]{:S(2)}, u32[]{:S(2)}) async-start(f16[32,48,128]{2,1,0:T(8,128)(2,1)} %copy.10), calls=%async_computation.3 | async-start | bytes 786432 | tf_op jit(solution)/shard_map/all_to_all | solution.py:195
  122.9 0.0 collective-permute-done.6.refs_2_
  122.9 0.0 all-gather.2.cloned.1.call-done
  123.0 0.0 copy-start
  123.0 1.9 %copy-done = bf16[4096,384]{1,0:T(8,128)(2,1)S(1)} copy-done((bf16[4096,384]{1,0:T(8,128)(2,1)S(1)}, bf16[4096,384]{1,0:T(8,128)(2,1)}, u32[]{:S(2)}) %copy-start) | copy-done | bytes 3145752
  124.9 0.0 copy-start.1
  124.9 3.3 %project.1 = (f32[128,192]{1,0:T(8,128)S(1)}, f32[144,192]{1,0:T(8,128)S(1)}) custom-call(s32[1]{0:T(128)} %bitcast.8.zh_ref, s32[16]{0:T(128)S(1)} %xor.16.place_ref, bf16[2,16,128,384]{3,2,1,0:T(8,128)(2,1)S(1)} %bitcast.14, bf16[4,192,384]{2,1,0:T(8,128)(2,1)S(1)} %pad_maximum_fusion.refs_0_, bf16[4,192,384]{2,1,0:T(8,128)(2,1)S(1)} %collective-permute-done.4.refs_1_, ...), custom_call_target="tpu_custom_call" | custom-call | flops 999999995904 | bytes 6291456 | tf_op jit(solution)/shard_map/project/pallas_call | solution.py:160
  128.2 12.0 %collective-permute-start.7 = (f16[144,192]{1,0:T(8,128)(2,1)S(1)}, f16[144,192]{1,0:T(8,128)(2,1)S(1)}, u32[]{:S(2)}, u32[]{:S(2)}) collective-permute-start(f16[144,192]{1,0:T(8,128)(2,1)S(1)} %convert_element_type.22), channel_id=1, source_target_pairs={{0,16},{16,0},{1,17},{17,1},{2,18},{18,2},{3,19},{19,3},{4,20},{20... | collective-permute-start | bytes 165896 | tf_op jit(solution)/shard_map/ppermute | solution.py:252
  140.2 0.0 copy-done.1
  140.2 11.1 %all-to-all-done.3 = f16[32,48,128]{2,1,0:T(8,128)(2,1)} async-done(((f16[32,48,128]{2,1,0:T(8,128)(2,1)}), f16[32,48,128]{2,1,0:T(8,128)(2,1)}, u32[]{:S(2)}, u32[]{:S(2)}) %all-to-all-start.3) | async-done | bytes 393248 | tf_op jit(solution)/shard_map/all_to_all | solution.py:195
  151.3 1.0 convert_element_type.21.x_ref
  152.3 0.6 unpack.1
  153.0 1.3 copy.11
  154.3 3.1 %collective-permute-done.7 = f16[144,192]{1,0:T(8,128)(2,1)S(1)} collective-permute-done((f16[144,192]{1,0:T(8,128)(2,1)S(1)}, f16[144,192]{1,0:T(8,128)(2,1)S(1)}, u32[]{:S(2)}, u32[]{:S(2)}) %collective-permute-start.7) | collective-permute-done | bytes 55328 | tf_op jit(solution)/shard_map/ppermute | solution.py:252
  157.4 0.5 slice.9
  158.6 0.8 pad_maximum_fusion.1
  (7 shorter events, 0.1 us)
Async XLA Ops:
  7.2 28.9 %collective-permute-start = (bf16[192,384]{1,0:T(8,128)(2,1)}, bf16[192,384]{1,0:T(8,128)(2,1)S(1)}, u32[]{:S(2)}, u32[]{:S(2)}) collective-permute-start(bf16[192,384]{1,0:T(8,128)(2,1)} %param.5), channel_id=1, source_target_pairs={{0,0},{1,32},{2,64},{3,96},{4,128},{5,160},{6,192},{7,224},{8,256}... | collective-permute-start | bytes 442376 | tf_op jit(solution)/shard_map/ppermute | solution.py:216
  13.9 47.8 %all-to-all-start = ((bf16[32,48,128]{2,1,0:T(8,128)(2,1)}), bf16[32,48,128]{2,1,0:T(8,128)(2,1)S(1)}, u32[]{:S(2)}, u32[]{:S(2)}) async-start(bf16[32,48,128]{2,1,0:T(8,128)(2,1)} %reshape.104), calls=%async_computation | async-start | bytes 786432 | tf_op jit(solution)/shard_map/all_to_all | solution.py:195
  33.7 89.3 %all-gather.2.cloned.1.call-start = ((), (), s32[]{:S(2)}) async-start(), calls=%async_computation.4 | async-start | bytes 3244032 | tf_op jit(solution)/shard_map/all_gather | solution.py:230
  36.0 8.4 %collective-permute-start.1 = (bf16[192,384]{1,0:T(8,128)(2,1)S(1)}, bf16[192,384]{1,0:T(8,128)(2,1)S(1)}, u32[]{:S(2)}, u32[]{:S(2)}) collective-permute-start(bf16[192,384]{1,0:T(8,128)(2,1)S(1)} %relay.1), channel_id=1, source_target_pairs={{0,32},{32,64},{64,96},{96,0},{1,33},{33,65},{65,97},{97,1},{2,34}... | collective-permute-start | bytes 442376 | tf_op jit(solution)/shard_map/ppermute | solution.py:199
  38.0 7.7 %collective-permute-start.2 = (bf16[192,384]{1,0:T(8,128)(2,1)S(1)}, bf16[192,384]{1,0:T(8,128)(2,1)S(1)}, u32[]{:S(2)}, u32[]{:S(2)}) collective-permute-start(bf16[192,384]{1,0:T(8,128)(2,1)S(1)} %relay.1), channel_id=1, source_target_pairs={{0,64},{32,96},{64,0},{96,32},{1,65},{33,97},{65,1},{97,33},{2,66}... | collective-permute-start | bytes 442376 | tf_op jit(solution)/shard_map/ppermute | solution.py:199
  39.9 8.0 %collective-permute-start.3 = (bf16[192,384]{1,0:T(8,128)(2,1)S(1)}, bf16[192,384]{1,0:T(8,128)(2,1)S(1)}, u32[]{:S(2)}, u32[]{:S(2)}) collective-permute-start(bf16[192,384]{1,0:T(8,128)(2,1)S(1)} %relay.1), channel_id=1, source_target_pairs={{0,96},{32,0},{64,32},{96,64},{1,97},{33,1},{65,33},{97,65},{2,98}... | collective-permute-start | bytes 442376 | tf_op jit(solution)/shard_map/ppermute | solution.py:199
  63.2 19.4 %all-to-all-start.1 = ((f32[16,80,128]{2,1,0:T(8,128)}), f32[16,80,128]{2,1,0:T(8,128)S(1)}, u32[]{:S(2)}, u32[]{:S(2)}) async-start(f32[16,80,128]{2,1,0:T(8,128)} %bitcast), calls=%async_computation.1 | async-start | bytes 1310720 | tf_op jit(solution)/shard_map/all_to_all | solution.py:195
  70.3 26.4 %collective-permute-start.4 = (bf16[4,192,384]{2,1,0:T(8,128)(2,1)S(1)}, bf16[4,192,384]{2,1,0:T(8,128)(2,1)S(1)}, u32[]{:S(2)}, u32[]{:S(2)}) collective-permute-start(bf16[4,192,384]{2,1,0:T(8,128)(2,1)S(1)} %pad_maximum_fusion.refs_0_), channel_id=1, source_target_pairs={{0,128},{128,256},{256,384},{384,0},{1,129},{129,257},{257,385},{3... | collective-permute-start | bytes 1769480 | tf_op jit(solution)/shard_map/ppermute | solution.py:199
  73.6 24.5 %collective-permute-start.5 = (bf16[4,192,384]{2,1,0:T(8,128)(2,1)S(1)}, bf16[4,192,384]{2,1,0:T(8,128)(2,1)S(1)}, u32[]{:S(2)}, u32[]{:S(2)}) collective-permute-start(bf16[4,192,384]{2,1,0:T(8,128)(2,1)S(1)} %pad_maximum_fusion.refs_0_), channel_id=1, source_target_pairs={{0,384},{128,0},{256,128},{384,256},{1,385},{129,1},{257,129},{385... | collective-permute-start | bytes 1769480 | tf_op jit(solution)/shard_map/ppermute | solution.py:199
  83.5 16.9 %all-to-all-start.2 = ((f32[16,80,128]{2,1,0:T(8,128)}), f32[16,80,128]{2,1,0:T(8,128)S(1)}, u32[]{:S(2)}, u32[]{:S(2)}) async-start(f32[16,80,128]{2,1,0:T(8,128)} %sum_and_repeat.1), calls=%async_computation.2 | async-start | bytes 1310720 | tf_op jit(solution)/shard_map/all_to_all | solution.py:195
  100.6 22.4 %collective-permute-start.6 = (bf16[4,192,384]{2,1,0:T(8,128)(2,1)S(1)}, bf16[4,192,384]{2,1,0:T(8,128)(2,1)}, u32[]{:S(2)}, u32[]{:S(2)}) collective-permute-start(bf16[4,192,384]{2,1,0:T(8,128)(2,1)S(1)} %collective-permute-done.4.refs_1_), channel_id=1, source_target_pairs={{0,128},{128,256},{256,384},{384,0},{1,129},{129,257},{257,385},{3... | collective-permute-start | bytes 1769480 | tf_op jit(solution)/shard_map/ppermute | solution.py:199
  113.0 38.3 %all-to-all-start.3 = ((f16[32,48,128]{2,1,0:T(8,128)(2,1)}), f16[32,48,128]{2,1,0:T(8,128)(2,1)}, u32[]{:S(2)}, u32[]{:S(2)}) async-start(f16[32,48,128]{2,1,0:T(8,128)(2,1)} %copy.10), calls=%async_computation.3 | async-start | bytes 786432 | tf_op jit(solution)/shard_map/all_to_all | solution.py:195
  123.0 1.9 %copy-start = (bf16[4096,384]{1,0:T(8,128)(2,1)S(1)}, bf16[4096,384]{1,0:T(8,128)(2,1)}, u32[]{:S(2)}) copy-start(bf16[4096,384]{1,0:T(8,128)(2,1)} %all-gather.2.cloned.1.call-done) | copy-start | bytes 9437188
  124.9 15.3 %copy-start.1 = (f32[32]{0:T(128)S(1)}, f32[32]{0:T(128)}, u32[]{:S(2)}) copy-start(f32[32]{0:T(128)} %abs_reduce_fusion.1) | copy-start | bytes 388
  128.2 29.2 %collective-permute-start.7 = (f16[144,192]{1,0:T(8,128)(2,1)S(1)}, f16[144,192]{1,0:T(8,128)(2,1)S(1)}, u32[]{:S(2)}, u32[]{:S(2)}) collective-permute-start(f16[144,192]{1,0:T(8,128)(2,1)S(1)} %convert_element_type.22), channel_id=1, source_target_pairs={{0,16},{16,0},{1,17},{17,1},{2,18},{18,2},{3,19},{19,3},{4,20},{20... | collective-permute-start | bytes 165896 | tf_op jit(solution)/shard_map/ppermute | solution.py:252
Sparse Core Ops, SparseCore 0:
  36.7 74.1 all-gather.1
